TPU v7x, 512 devices: a whole 4x8x8 slice. The times are simulated.
512 devices in a mesh: grp: 4 (over x), row: 128 (over z, y, core).
Axes of the slice: x: 4, y: 8, z: 8, core: 2. Of those that a mesh axis runs over, the one named last changes fastest.
Arguments:
- pressure: float32 [1, 1048576], P(None, ('grp', 'row')), may hold values from -6 to 6
- mic_cycle: int32 [1, 1048576], P(None, ('grp', 'row')), may hold values from 0 to 4095, as said below
- mic_azimuth: int32 [1, 1048576], P(None, ('grp', 'row')), may hold values from 0 to 8191
- bin_index: int32 [1], replicated, may hold values from 0 to 15
- source_cell: int32 [512], replicated, may hold values from 0 to 999, as said below
Outputs:
- strengths: float32 [1, 512], P(None, 'grp')
Inputs may be any that keep to these rules, and one draw needn't show every extreme that they name: `source_cell`: distinct cells of a 10 x 10 x 10 grid. `mic_cycle`: within each bin, never falling along the sample axis.
All inputs are finite; a program needn't handle non-finite values.
Results may differ from a plain program's by a relative error of at most 0.0003.
Values sent between devices are 32-bit elements; how exact they have to be, the bound alone decides.
A program may use at most 64 MiB of HBM per device.

v0:
```python
import jax
import jax.numpy as jnp
from jax import lax
from jax.sharding import PartitionSpec as P

NRING = 4096
NAZ = 8192


ridge = 0.5
spacing = 0.08


def from_partner(value, axis, apart):
    mask = 2**apart
    pairs = [(source, source ^ mask) for source in range(lax.axis_size(axis))]
    return lax.ppermute(value, axis, pairs)


def source_points(source_cell):
    layer_i = (source_cell // 100).astype(jnp.float32)
    layer_j = (source_cell // 10 % 10).astype(jnp.float32)
    layer_l = (source_cell % 10).astype(jnp.float32)
    return (spacing * (layer_i - 4.5), spacing * (layer_j - 4.5), spacing * (layer_l - 4.5))


def green_block(cycle_idx, azim_idx, points, wavenum):
    polar = jnp.pi * (cycle_idx.astype(jnp.float32) + 0.5) / NRING
    azimuth = 2.0 * jnp.pi * azim_idx.astype(jnp.float32) / NAZ
    mic_x = jnp.sin(polar) * jnp.cos(azimuth)
    mic_y = jnp.sin(polar) * jnp.sin(azimuth)
    mic_z = jnp.cos(polar)
    delta_x = mic_x[..., None] - points[0]
    delta_y = mic_y[..., None] - points[1]
    delta_z = mic_z[..., None] - points[2]
    dist = jnp.sqrt(delta_x * delta_x + delta_y * delta_y + delta_z * delta_z)
    return jnp.cos(wavenum[:, None, None] * dist) / dist


def outer_self(factor):
    return jnp.einsum("fij,fkj->fik", factor, factor, precision=lax.Precision.HIGHEST)


def solve_batch(factor, vector):
    middle = lax.linalg.triangular_solve(factor, vector[..., None], left_side=True, lower=True)
    result = lax.linalg.triangular_solve(
        factor, middle, left_side=True, lower=True, transpose_a=True
    )
    return result[..., 0]


def shards(pressure, mic_cycle, mic_azimuth, bin_index, source_cell):
    points = source_points(source_cell)
    wavenum = 1.5 * (bin_index.astype(jnp.float32) + 1.0)
    fbins, local_rows = pressure.shape
    width = source_cell.shape[0]
    block_rows = min(local_rows, 512)
    blocks = local_rows // block_rows

    def regroup(array):
        return jnp.moveaxis(array.reshape(fbins, blocks, block_rows), 1, 0)

    def step(carry, items):
        gram_acc, rhs_acc = carry
        press_blk, cycle_blk, azim_blk = items
        panel = green_block(cycle_blk, azim_blk, points, wavenum)
        gram_acc = gram_acc + jnp.einsum(
            "fms,fmt->fst", panel, panel, precision=lax.Precision.HIGHEST
        )
        rhs_acc = rhs_acc + jnp.einsum(
            "fms,fm->fs", panel, press_blk, precision=lax.Precision.HIGHEST
        )
        return ((gram_acc, rhs_acc), None)

    start = (jnp.zeros((fbins, width, width), jnp.float32), jnp.zeros((fbins, width), jnp.float32))
    (gram_part, rhs_part), _ = lax.scan(
        step, start, (regroup(pressure), regroup(mic_cycle), regroup(mic_azimuth))
    )
    groups = lax.axis_size("grp")
    total_rows = local_rows * groups * lax.axis_size("row")
    root_rows = jnp.sqrt(jnp.float32(total_rows))
    identity_mat = jnp.eye(width, dtype=jnp.float32)
    group_gram, group_rhs = lax.psum((gram_part, rhs_part), "row")
    lower = jnp.linalg.cholesky(group_gram / total_rows + ridge / groups * identity_mat)
    rhs = group_rhs / root_rows
    for level in range(groups.bit_length() - 1):
        other_lower, other_rhs = from_partner((lower, rhs), "grp", level)
        lower = jnp.linalg.cholesky(outer_self(lower) + outer_self(other_lower))
        rhs = rhs + other_rhs
    solved = solve_batch(lower, rhs)
    share = width // groups
    offset = lax.axis_index("grp") * share
    return lax.dynamic_slice_in_dim(solved, offset, share, 1)


def solution(mesh):
    placed = (P(None, ("grp", "row")), P(None, ("grp", "row")), P(None, ("grp", "row")), P(), P())
    return jax.shard_map(
        shards, mesh=mesh, in_specs=placed, out_specs=P(None, "grp"), check_vma=False
    )
```

profile of v0, /device:TPU:1, one launch (start us, length us, event | category | flops | bytes accessed | tf_op | source)
XLA Modules:
  0.0 879.2 jit_solution(10173922836038595339)
XLA Ops:
  7.9 65.9 %while.18 = (s32[]{:T(128)}, f32[1,512,512]{2,1,0:T(8,128)S(1)}, f32[1,512]{1,0:T(1,128)S(1)}, f32[1]{0:T(128)}, s32[4,1,512]{2,1,0:T(1,128)}, /*index=5*/s32[4,...) while((s32[]{:T(128)}, f32[1,512,512]{2,1,0:T(8,128)S(1)}, ...), condition=%wide.region_1.2_spmd.clone, body=%wide.region_0.1_spmd.clone.sunk | while | flops 1619530240 | bytes 2139272 | solution.py:76
  8.8 10.2 %fusion.124 = f32[1,512,512]{2,1,0:T(8,128)S(1)} fusion(f32[1,512,512]{2,1,0:T(8,128)S(1)} %get-tuple-element.384, f32[512]{0:T(512)S(1)} %get-tuple-element.403, f32[512]{0:T(512)S(1)} %bitcast.425, f32[512]{0:T(512)S(1)} %get-tuple-element.402, f32[512]{0:T(512)S(1)} %bitcast.423, f32[512]{0:T(512)S(1)} %get-tuple-element.401, ...), kind=kOutput, calls=%fused_computation.3.clone.1 | convolution fusion | flops 1613758464 | bytes 2109445 | tf_op jit(solution)/shard_map/while/body/eval_jaxpr/fms,fmt->fst/dot_general | solution.py:67
  25.2 10.2 %fusion.124 = f32[1,512,512]{2,1,0:T(8,128)S(1)} fusion(f32[1,512,512]{2,1,0:T(8,128)S(1)} %get-tuple-element.384, f32[512]{0:T(512)S(1)} %get-tuple-element.403, f32[512]{0:T(512)S(1)} %bitcast.425, f32[512]{0:T(512)S(1)} %get-tuple-element.402, f32[512]{0:T(512)S(1)} %bitcast.423, f32[512]{0:T(512)S(1)} %get-tuple-element.401, ...), kind=kOutput, calls=%fused_computation.3.clone.1 | convolution fusion | flops 1613758464 | bytes 2109445 | tf_op jit(solution)/shard_map/while/body/eval_jaxpr/fms,fmt->fst/dot_general | solution.py:67
  41.6 10.2 %fusion.124 = f32[1,512,512]{2,1,0:T(8,128)S(1)} fusion(f32[1,512,512]{2,1,0:T(8,128)S(1)} %get-tuple-element.384, f32[512]{0:T(512)S(1)} %get-tuple-element.403, f32[512]{0:T(512)S(1)} %bitcast.425, f32[512]{0:T(512)S(1)} %get-tuple-element.402, f32[512]{0:T(512)S(1)} %bitcast.423, f32[512]{0:T(512)S(1)} %get-tuple-element.401, ...), kind=kOutput, calls=%fused_computation.3.clone.1 | convolution fusion | flops 1613758464 | bytes 2109445 | tf_op jit(solution)/shard_map/while/body/eval_jaxpr/fms,fmt->fst/dot_general | solution.py:67
  58.0 10.2 %fusion.124 = f32[1,512,512]{2,1,0:T(8,128)S(1)} fusion(f32[1,512,512]{2,1,0:T(8,128)S(1)} %get-tuple-element.384, f32[512]{0:T(512)S(1)} %get-tuple-element.403, f32[512]{0:T(512)S(1)} %bitcast.425, f32[512]{0:T(512)S(1)} %get-tuple-element.402, f32[512]{0:T(512)S(1)} %bitcast.423, f32[512]{0:T(512)S(1)} %get-tuple-element.401, ...), kind=kOutput, calls=%fused_computation.3.clone.1 | convolution fusion | flops 1613758464 | bytes 2109445 | tf_op jit(solution)/shard_map/while/body/eval_jaxpr/fms,fmt->fst/dot_general | solution.py:67
  74.9 201.1 %all-reduce.3.cloned.1.call-done = f32[1,512,512]{2,1,0:T(8,128)} async-done(((f32[1,512,512]{2,1,0:T(8,128)}), f32[1,512,512]{2,1,0:T(8,128)}) %all-reduce.3.cloned.1.call-update) | async-done | bytes 1048592 | tf_op jit(solution)/shard_map/psum | solution.py:83
  278.9 11.7 %custom-call.46 = f32[1,128,128]{2,1,0:T(8,128)S(1)} custom-call(f32[1,128,128]{2,1,0:T(8,128)S(1)} %copy.21), custom_call_target="Cholesky" | custom-call | tf_op jit(solution)/shard_map/jit(cholesky)/cholesky | solution.py:84
  290.6 9.8 %custom-call.47 = f32[1,1,128,128]{2,3,1,0:T(8,128)S(1)} custom-call(f32[1,1,128,128]{3,2,1,0:T(8,128)S(1)} %get-tuple-element.263), custom_call_target="InvertDiagBlocksLowerTriangular" | custom-call | tf_op jit(solution)/shard_map/jit(cholesky)/cholesky | solution.py:84
  301.6 11.7 %custom-call.48 = f32[1,128,128]{2,1,0:T(8,128)S(1)} custom-call(f32[1,128,128]{2,1,0:T(8,128)S(1)} %copy.23), custom_call_target="Cholesky" | custom-call | tf_op jit(solution)/shard_map/jit(cholesky)/cholesky | solution.py:84
  313.3 10.2 %custom-call.49 = f32[1,1,128,128]{2,3,1,0:T(8,128)S(1)} custom-call(f32[1,1,128,128]{3,2,1,0:T(8,128)S(1)} %get-tuple-element.260), custom_call_target="InvertDiagBlocksLowerTriangular" | custom-call | tf_op jit(solution)/shard_map/jit(cholesky)/cholesky | solution.py:84
  324.4 11.7 %custom-call.50 = f32[1,128,128]{2,1,0:T(8,128)S(1)} custom-call(f32[1,128,128]{2,1,0:T(8,128)S(1)} %copy.25), custom_call_target="Cholesky" | custom-call | tf_op jit(solution)/shard_map/jit(cholesky)/cholesky | solution.py:84
  347.5 11.9 %custom-call.52 = f32[1,128,128]{2,1,0:T(8,128)S(1)} custom-call(f32[1,128,128]{2,1,0:T(8,128)S(1)} %copy.27), custom_call_target="Cholesky" | custom-call | tf_op jit(solution)/shard_map/jit(cholesky)/cholesky | solution.py:84
  366.5 247.8 %psum.15 = f32[1,512]{1,0:T(1,128)S(1)} all-reduce(f32[1,512]{1,0:T(1,128)S(1)} %get-tuple-element.159), channel_id=1, replica_groups=mesh['grp'=4,'row'=128] {'row'}, use_global_device_ids=true, to_apply=%region_11.13 | all-reduce | flops 512 | bytes 4096 | tf_op jit(solution)/shard_map/psum | solution.py:83
  618.7 11.7 %custom-call.53 = f32[1,128,128]{2,1,0:T(8,128)S(1)} custom-call(f32[1,128,128]{2,1,0:T(8,128)S(1)} %cholesky.596), custom_call_target="Cholesky" | custom-call | tf_op jit(solution)/shard_map/jit(cholesky)/cholesky | solution.py:88
  630.6 9.8 %custom-call.54 = f32[1,1,128,128]{2,3,1,0:T(8,128)S(1)} custom-call(f32[1,1,128,128]{3,2,1,0:T(8,128)S(1)} %get-tuple-element.253), custom_call_target="InvertDiagBlocksLowerTriangular" | custom-call | tf_op jit(solution)/shard_map/jit(cholesky)/cholesky | solution.py:88
  641.0 12.1 %custom-call.55 = f32[1,128,128]{2,1,0:T(8,128)S(1)} custom-call(f32[1,128,128]{2,1,0:T(8,128)S(1)} %cholesky.600), custom_call_target="Cholesky" | custom-call | tf_op jit(solution)/shard_map/jit(cholesky)/cholesky | solution.py:88
  665.0 11.7 %custom-call.57 = f32[1,128,128]{2,1,0:T(8,128)S(1)} custom-call(f32[1,128,128]{2,1,0:T(8,128)S(1)} %cholesky.605), custom_call_target="Cholesky" | custom-call | tf_op jit(solution)/shard_map/jit(cholesky)/cholesky | solution.py:88
  687.8 11.9 %custom-call.59 = f32[1,128,128]{2,1,0:T(8,128)S(1)} custom-call(f32[1,128,128]{2,1,0:T(8,128)S(1)} %fusion.21), custom_call_target="Cholesky" | custom-call | tf_op jit(solution)/shard_map/jit(cholesky)/cholesky | solution.py:88
  709.4 17.1 %collective-permute-done.2 = f32[1,512]{1,0:T(1,128)S(1)} collective-permute-done((f32[1,512]{1,0:T(1,128)S(1)}, f32[1,512]{1,0:T(1,128)S(1)}, u32[]{:S(2)}, u32[]{:S(2)}) %collective-permute-start.2) | collective-permute-done | bytes 2080 | tf_op jit(solution)/shard_map/ppermute | solution.py:17
  736.6 11.7 %custom-call.60 = f32[1,128,128]{2,1,0:T(8,128)S(1)} custom-call(f32[1,128,128]{2,1,0:T(8,128)S(1)} %cholesky.609), custom_call_target="Cholesky" | custom-call | tf_op jit(solution)/shard_map/jit(cholesky)/cholesky | solution.py:88
  759.0 11.9 %custom-call.62 = f32[1,128,128]{2,1,0:T(8,128)S(1)} custom-call(f32[1,128,128]{2,1,0:T(8,128)S(1)} %cholesky.613), custom_call_target="Cholesky" | custom-call | tf_op jit(solution)/shard_map/jit(cholesky)/cholesky | solution.py:88
  782.7 11.7 %custom-call.64 = f32[1,128,128]{2,1,0:T(8,128)S(1)} custom-call(f32[1,128,128]{2,1,0:T(8,128)S(1)} %cholesky.618), custom_call_target="Cholesky" | custom-call | tf_op jit(solution)/shard_map/jit(cholesky)/cholesky | solution.py:88
  805.8 11.7 %custom-call.66 = f32[1,128,128]{2,1,0:T(8,128)S(1)} custom-call(f32[1,128,128]{2,1,0:T(8,128)S(1)} %fusion.22), custom_call_target="Cholesky" | custom-call | tf_op jit(solution)/shard_map/jit(cholesky)/cholesky | solution.py:88
  829.1 39.3 %custom-call.29 = f32[1,4,128,128]{2,3,1,0:T(8,128)S(1)} custom-call(f32[1,4,128,128]{3,2,1,0:T(8,128)S(1)} %bitcast.437), custom_call_target="InvertDiagBlocksLowerTriangular" | custom-call | tf_op jit(solution)/shard_map/triangular_solve | solution.py:46
  (137 shorter events, 146.9 us)
Async XLA Ops:
  6.5 0.7 copy-start.2
  6.5 269.4 %all-reduce.3.cloned.1.call-start = ((), (), s32[]{:S(2)}) async-start(), calls=%async_computation | async-start | bytes 2097152 | tf_op jit(solution)/shard_map/psum | solution.py:83
  73.8 1.0 copy-start.1
  277.3 1.2 copy-start
  363.4 252.8 %collective-permute-start = (f32[1,512,512]{2,1,0:T(8,128)S(1)}, f32[1,512,512]{2,1,0:T(8,128)S(1)}, u32[]{:S(2)}, u32[]{:S(2)}) collective-permute-start(f32[1,512,512]{2,1,0:T(8,128)S(1)} %select_select_fusion.2), channel_id=1, source_target_pairs={{0,128},{128,0},{256,384},{384,256},{1,129},{129,1},{257,385},{385... | collective-permute-start | bytes 3145736 | tf_op jit(solution)/shard_map/ppermute | solution.py:17
  703.1 31.0 %collective-permute-start.1 = (f32[1,512,512]{2,1,0:T(8,128)S(1)}, f32[1,512,512]{2,1,0:T(8,128)S(1)}, u32[]{:S(2)}, u32[]{:S(2)}) collective-permute-start(f32[1,512,512]{2,1,0:T(8,128)S(1)} %select_select_fusion.1), channel_id=1, source_target_pairs={{0,256},{128,384},{256,0},{384,128},{1,257},{129,385},{257,1},{385... | collective-permute-start | bytes 3145736 | tf_op jit(solution)/shard_map/ppermute | solution.py:17
  707.4 19.0 %collective-permute-start.2 = (f32[1,512]{1,0:T(1,128)S(1)}, f32[1,512]{1,0:T(1,128)S(1)}, u32[]{:S(2)}, u32[]{:S(2)}) collective-permute-start(f32[1,512]{1,0:T(1,128)S(1)} %broadcast_multiply_fusion), channel_id=1, source_target_pairs={{0,128},{128,0},{256,384},{384,256},{1,129},{129,1},{257,385},{385... | collective-permute-start | bytes 6152 | tf_op jit(solution)/shard_map/ppermute | solution.py:17
  726.4 5.8 collective-permute-start.3
Sparse Core Ops, SparseCore 0:
  75.0 200.9 all-reduce.2
where the time goes:
time: 896 us; the launch traced here: 879 us
  other arithmetic  284 us (32%)
  blocking collectives  248 us (28%)
  waiting for transfers between devices  221 us (25%)
  matrix products  78.7 us (9%)
  between operations  22.9 us (3%)
  starting transfers between devices  12.7 us (1%)
  local copies, waits for them, and re-layouts  12.4 us (1%)
    psum x1, blocking collectives, shards(): group_gram, group_rhs = lax.psum((gram_part, rhs_part), 'row')  248 us
    psum x1, waiting for transfers between devices, shards(): group_gram, group_rhs = lax.psum((gram_part, rhs_part), 'row')  201 us
    another operation x30, other arithmetic, shards(): lower = jnp.linalg.cholesky(outer_self(lower) + outer_self(other_lower))  159 us
    another operation x14, other arithmetic, shards(): jnp.linalg.cholesky(group_gram / total_rows + ridge / groups * identity_mat)  79 us
    dot_general x4, matrix products, step(): jnp.einsum('fms,fmt->fst', panel, panel, precision=lax.Precision.HIGHEST)  40.7 us
    another operation x3, other arithmetic, solve_batch(): lax.linalg.triangular_solve(factor, middle, left_side=True, lower=True, t...  39.4 us
    dot_general x4, matrix products, step(): jnp.einsum('fms,fm->fs', panel, press_blk, precision=lax.Precision.HIGHEST)  21.6 us
    ppermute x4, waiting for transfers between devices, from_partner(): return lax.ppermute(value, axis, pairs)  19.5 us
  transfers between devices with their start and end apart: 5, of which 3 were waited for; matrix products, arithmetic and copies ran while one was open for 0% of the time, Pallas kernels for 0%

commit v1 on v0

v1 whole, which is shorter than its diff:
```python
import functools

import jax
import jax.numpy as jnp
import numpy as np
from jax import lax
from jax.experimental import pallas as pl
from jax.experimental.pallas import tpu as pltpu
from jax.sharding import PartitionSpec as P

F32 = jnp.float32
BF = jnp.bfloat16
S = 512
NRING = 4096
NAZ = 8192
PAIRS = [(i, j) for i in range(4) for j in range(i, 4)]

NT=(((1,),(1,)),((),()))
CHUNK=256
COS=[float(v) for v in (6.283185307179586,-41.34170224039975,81.60524927607504,-76.70585975306136,42.05869394489765)]
MAGIC=12582912.0

def split(v,n):
    parts=[]
    for _ in range(n-1):
        h=v.astype(BF); parts.append(h); v=v-h.astype(F32)
    parts.append(v.astype(BF)); return parts

def cos_turns(t, gain=None):
    y=t-((t+MAGIC)-MAGIC)
    v=0.25-jnp.abs(y)
    u=v*v
    s=COS[4]
    for c in COS[3::-1]: s=s*u+c
    return (s*v) if gain is None else s*(v*gain)

def panel_kernel(spacing, bin_ref, p_ref, cyc_ref, az_ref, src_ref, out_ref, src_scr, mic_scr, hi_scr, lo_scr):
    cell=src_ref[...].astype(F32)
    li=jnp.floor((cell+0.5)*0.01); rest=cell-100.0*li
    lj=jnp.floor((rest+0.5)*0.1); ll=rest-10.0*lj
    t=[2.0*v-9.0 for v in (li,lj,ll)]
    sq=t[0]*t[0]+t[1]*t[1]+t[2]*t[2]
    one=jnp.ones_like(sq); zero=jnp.zeros_like(sq)
    rows=[t[0]]*3+[t[1]]*3+[t[2]]*3+[sq]*3+[one]
    sT=jnp.concatenate(rows+[zero]*(128-len(rows)),axis=0)
    src_scr[...]=sT.T.astype(BF)
    half=spacing*0.5
    polar=(2*cyc_ref[...]+1).astype(F32)*(1.0/16384.0)
    azim=az_ref[...].astype(F32)*(1.0/8192.0)
    sp=cos_turns(polar-0.25); cp=cos_turns(polar)
    mic=[sp*cos_turns(azim), sp*cos_turns(azim-0.25), cp]
    mrows=[]
    for m in mic: mrows+=split(m*(-2.0*half),3)
    w=jnp.full(mic[0].shape,half*half,F32)
    mrows+=split(w,3)+[jnp.ones_like(w).astype(BF)]
    mrows=[m.astype(F32) for m in mrows]
    mrows+=[jnp.zeros_like(w)]*(16-len(mrows))
    mic_scr[...]=jnp.concatenate(mrows,axis=0).astype(BF)
    n=p_ref.shape[1]
    ph,pm=[v.astype(F32) for v in split(p_ref[...],2)]
    hi_scr[S:S+16,:]=jnp.concatenate([ph,pm]+[jnp.zeros_like(ph)]*14,axis=0).astype(BF)
    kc=1.5*(bin_ref[0].astype(F32)+1.0)*float(1/(2*np.pi))
    for c in range(n//CHUNK):
        cols=slice(c*CHUNK,(c+1)*CHUNK)
        d2=jnp.dot(src_scr[:,:16],mic_scr[:,cols],preferred_element_type=F32)
        r=lax.rsqrt(d2)
        val=cos_turns((d2*r)*kc, r)
        h=val.astype(BF)
        hi_scr[0:S,cols]=h
        lo_scr[:,cols]=(val-h.astype(F32)).astype(BF)
    H=lax.dot_general(hi_scr[...],hi_scr[0:S,:],NT,preferred_element_type=F32)
    L=lax.dot_general(hi_scr[...],lo_scr[...],NT,preferred_element_type=F32)
    nblk=0
    for i in range(4):
        for j in range(i,4):
            a=slice(128*i,128*i+128); b=slice(128*j,128*j+128)
            out_ref[128*nblk:128*nblk+128,:]=H[a,b]+L[a,b]+L[b,a].T
            nblk+=1
    r=(H[S:S+1]+L[S:S+1])+(H[S+1:S+2]+L[S+1:S+2])
    tail=jnp.concatenate([r[:,128*i:128*i+128] for i in range(4)]+[jnp.zeros((4,128),F32)],axis=0)
    out_ref[1280:1288,:]=tail
    out_ref[1288:1536,:]=jnp.zeros((248,128),F32)

def panel(spacing, p, cyc, az, b, src):
    n=p.shape[1]
    V=pl.BlockSpec(memory_space=pltpu.VMEM)
    return pl.pallas_call(functools.partial(panel_kernel,spacing),
        out_shape=jax.ShapeDtypeStruct((1536,128),F32),
        in_specs=[pl.BlockSpec(memory_space=pltpu.SMEM),V,V,V,V],out_specs=V,
        scratch_shapes=[pltpu.VMEM((S,128),BF),pltpu.VMEM((16,n),BF),pltpu.VMEM((S+16,n),BF),pltpu.VMEM((S,n),BF)],
        name="panel",compiler_params=pltpu.CompilerParams(vmem_limit_bytes=40<<20))(b,p,cyc,az,src.reshape(1,S))

MESH = pl.DeviceIdType.MESH


def reduce_kernel(nx, ny, nz, piece, in_ref, out_ref, acc_c, acc_x, acc_y, buf_c, buf_x, buf_y, buf_z,
                  send_c, recv_c, send_x, recv_x, send_y, recv_y, send_z, recv_z,
                  gsend_c, grecv_c, gsend_x, grecv_x, gsend_y, grecv_y):
    x = lax.axis_index("grp")
    row = lax.axis_index("row")
    c = lax.rem(row, 2)
    y = lax.rem(row // 2, ny)
    z = row // (2 * ny)
    def at_c(o):
        return {"row": row + lax.rem(c + o, 2) - c}
    def at_x(o):
        return {"grp": lax.rem(x + o, nx)}
    def at_y(o):
        return {"row": row + 2 * (lax.rem(y + o, ny) - y)}
    def at_z(o):
        return {"row": row + 2 * ny * (lax.rem(z + o, nz) - z)}
    partners = [at_c(1)] + [at_x(o) for o in range(1, nx)] + [at_y(o) for o in range(1, ny)]
    partners += [at_z(o) for o in range(1, nz)]
    barrier = pltpu.get_barrier_semaphore()
    for partner in partners:
        pl.semaphore_signal(barrier, inc=1, device_id=partner, device_id_type=MESH)
    pl.semaphore_wait(barrier, len(partners))

    def send(src, dst, ssem, rsem, partner):
        copy = pltpu.make_async_remote_copy(src_ref=src, dst_ref=dst, send_sem=ssem, recv_sem=rsem,
                                            device_id=partner, device_id_type=MESH)
        copy.start()
        return copy

    def rows(start, count):
        return pl.ds(pl.multiple_of(start, 8), count)

    row_y, row_x, row_c = piece, piece * ny, piece * ny * nx
    copy = send(in_ref.at[rows((1 - c) * row_c, row_c)], buf_c, send_c, recv_c, at_c(1))
    copy.wait()
    acc_c[...] = in_ref[rows(c * row_c, row_c), :] + buf_c[...]
    copies = [send(acc_c.at[rows(lax.rem(x + o, nx) * row_x, row_x)], buf_x.at[o - 1],
                   send_x.at[o - 1], recv_x.at[o - 1], at_x(o)) for o in range(1, nx)]
    for copy in copies:
        copy.wait()
    total = acc_c[rows(x * row_x, row_x), :]
    for o in range(1, nx):
        total = total + buf_x[o - 1]
    acc_x[...] = total
    copies = [send(acc_x.at[rows(lax.rem(y + o, ny) * row_y, row_y)], buf_y.at[o - 1],
                   send_y.at[o - 1], recv_y.at[o - 1], at_y(o)) for o in range(1, ny)]
    for copy in copies:
        copy.wait()
    total = acc_x[rows(y * row_y, row_y), :]
    for o in range(1, ny):
        total = total + buf_y[o - 1]
    acc_y[...] = total
    buf_z[z] = total
    copies = [send(acc_y, buf_z.at[z], send_z.at[o - 1], recv_z.at[o - 1], at_z(o)) for o in range(1, nz)]
    for copy in copies:
        copy.wait()
    total = buf_z[0]
    for o in range(1, nz):
        total = total + buf_z[o]
    mine = out_ref.at[rows(c * row_c + x * row_x + y * row_y, row_y)]
    mine[...] = total
    copies = [send(mine, mine, gsend_y.at[o - 1], grecv_y.at[o - 1], at_y(o)) for o in range(1, ny)]
    for copy in copies:
        copy.wait()
    mine = out_ref.at[rows(c * row_c + x * row_x, row_x)]
    copies = [send(mine, mine, gsend_x.at[o - 1], grecv_x.at[o - 1], at_x(o)) for o in range(1, nx)]
    for copy in copies:
        copy.wait()
    mine = out_ref.at[rows(c * row_c, row_c)]
    send(mine, mine, gsend_c, grecv_c, at_c(1)).wait()


def reduce_all(part, nx, ny, nz):
    piece = part.shape[0] // (2 * nx * ny)
    vmem = pl.BlockSpec(memory_space=pltpu.VMEM)
    dma = pltpu.SemaphoreType.DMA
    def pair(count):
        return [dma((count,)), dma((count,))]
    return pl.pallas_call(
        functools.partial(reduce_kernel, nx, ny, nz, piece),
        out_shape=jax.ShapeDtypeStruct(part.shape, F32),
        in_specs=[vmem],
        out_specs=vmem,
        scratch_shapes=[
            pltpu.VMEM((piece * ny * nx, 128), F32),
            pltpu.VMEM((piece * ny, 128), F32),
            pltpu.VMEM((piece, 128), F32),
            pltpu.VMEM((piece * ny * nx, 128), F32),
            pltpu.VMEM((nx - 1, piece * ny, 128), F32),
            pltpu.VMEM((ny - 1, piece, 128), F32),
            pltpu.VMEM((nz, piece, 128), F32),
            dma, dma, *pair(nx - 1), *pair(ny - 1), *pair(nz - 1),
            dma, dma, *pair(nx - 1), *pair(ny - 1),
        ],
        name="reduce_all",
        compiler_params=pltpu.CompilerParams(collective_id=0, has_side_effects=True, vmem_limit_bytes=32 << 20),
    )(part)

TERMS=6; SG=16; PAN=32; LEVEL=0
def dot(a,b): return jnp.dot(a,b,preferred_element_type=F32)
def mm(a,b):
    if TERMS==3:
        ah,am=split(a,2); bh,bm=split(b,2)
        return dot(jnp.concatenate([ah,am],1),jnp.concatenate([bh,bh],0))+dot(ah,bm)
    if TERMS==1:
        return dot(a.astype(BF),b.astype(BF))
    return jnp.dot(a,b,precision=lax.Precision.HIGHEST,preferred_element_type=F32)

def bl(v,c): return jnp.broadcast_to(v[:,c:c+1],(8,128))
def bs(v,r): return jnp.broadcast_to(v[r:r+1,:],(8,128))

def invert(M):
    lane=lax.broadcasted_iota(jnp.int32,(8,128),1); sub=lax.broadcasted_iota(jnp.int32,(8,128),0)
    biglane=lax.broadcasted_iota(jnp.int32,(128,128),1)
    nq=PAN//8
    for p in range(128//PAN):
        p0=PAN*p
        S=[M[p0+8*q:p0+8*q+8,:] for q in range(nq)]
        for h in range(PAN//SG):
            B=[[bl(S[q],p0+SG*h+j) for q in range(nq)] for j in range(SG)]
            for j in range(SG):
                row=SG*h+j; qj,rj=divmod(row,8); c=p0+row
                inv=1.0/bs(B[j][qj],rj)
                here=lane==c; mine=sub==rj
                prow=jnp.where(here,1.0,bs(S[qj],rj))*inv
                for j2 in range(j+1,SG):
                    raw=bs(B[j2][qj],rj); bp=raw*inv
                    for q in range(nq):
                        u=B[j2][q]-((B[j][q]*raw)*inv if j2==j+1 else B[j][q]*bp)
                        B[j2][q]=jnp.where(mine,bp,u) if q==qj else u
                for q in range(nq):
                    u=jnp.where(here,0.0,S[q])-B[j][q]*prow
                    S[q]=jnp.where(mine,prow,u) if q==qj else u
        R=jnp.concatenate(S,axis=0)
        pad=[jnp.zeros((PAN,128),F32)]*(128//PAN); pad[p]=R
        Rp=jnp.concatenate(pad,axis=0)
        upd=jnp.where((biglane>=p0)&(biglane<p0+PAN),0.0,M)-mm(M,Rp)
        M=jnp.concatenate([x for x in [upd[:p0],R,upd[p0+PAN:]] if x.shape[0]],axis=0)
    return M

def eliminate(mat):
    for k in range(4):
        b=128*k
        Mi=invert(mat[b:b+128,b:b+128])
        R=mm(Mi,mat[b:b+128,b+128:])
        order=[(k+1+t)%4 for t in range(3)]
        if k<3:
            o=k+1
            mat[128*o:128*o+128,128*o:128*o+128]-=mm(mat[128*o:128*o+128,b:b+128],R[:,:128])
            mat[128*o:128*o+128,128*o+128:]-=mm(mat[128*o:128*o+128,b:b+128],R[:,128:])
            order=order[1:]
        for o in order:
            mat[128*o:128*o+128,b+128:]-=mm(mat[128*o:128*o+128,b:b+128],R)
        mat[b:b+128,b+128:]=R

def assemble(red_ref, mat, scale, root, ridge):
    r=lax.broadcasted_iota(jnp.int32,(128,128),0); c=lax.broadcasted_iota(jnp.int32,(128,128),1)
    for n,(i,j) in enumerate(PAIRS):
        b=red_ref[128*n:128*n+128,:]*scale
        if i==j: b=b+jnp.where(r==c,ridge,0.0)
        mat[128*i:128*i+128,128*j:128*j+128]=b
        if i!=j: mat[128*j:128*j+128,128*i:128*i+128]=b.T
    for i in range(4):
        row=red_ref[1280+i:1281+i,:]*root
        mat[128*i:128*i+128,512:640]=jnp.broadcast_to(row,(128,128)).T

def solve_kernel(scale, root, ridge, axis, red_ref, out_ref, mat):
    assemble(red_ref, mat, scale, root, ridge)
    if LEVEL!=1: eliminate(mat)
    me=lax.axis_index(axis) if axis else 1
    blk=mat[pl.ds(pl.multiple_of(me*128,128),128),512:640]
    out_ref[...]=blk.T[0:1,:]

def solve(red, scale, root, ridge, axis):
    return pl.pallas_call(functools.partial(solve_kernel,scale,root,ridge,axis),
        out_shape=jax.ShapeDtypeStruct((1,128),jnp.float32),
        in_specs=[pl.BlockSpec(memory_space=pltpu.VMEM)],out_specs=pl.BlockSpec(memory_space=pltpu.VMEM),
        scratch_shapes=[pltpu.VMEM((512,640),jnp.float32)],name="solve",
        compiler_params=pltpu.CompilerParams(vmem_limit_bytes=32<<20))(red)


def shards(mesh, pressure, mic_cycle, mic_azimuth, bin_index, source_cell):
    nx = mesh.shape["grp"]
    ny = 8
    nz = mesh.shape["row"] // (2 * ny)
    count = pressure.shape[1] * nx * mesh.shape["row"]
    part = panel(0.08, pressure, mic_cycle, mic_azimuth, bin_index, source_cell)
    total = reduce_all(part, nx, ny, nz)
    return solve(total, 1.0 / count, 1.0 / count**0.5, 0.5, "grp")


def solution(mesh):
    placed = (P(None, ("grp", "row")), P(None, ("grp", "row")), P(None, ("grp", "row")), P(), P())
    return jax.shard_map(
        functools.partial(shards, mesh), mesh=mesh, in_specs=placed, out_specs=P(None, "grp"), check_vma=False
    )
```

time: 896 us -> 72.8 us (0.08); the launches traced: 879 us -> 72.5 us
  other arithmetic: 284 us -> 0 us
  blocking collectives: 248 us -> 0 us
  waiting for transfers between devices: 221 us -> 0 us
  matrix products: 78.7 us -> 0 us
  Pallas kernels: 0 us -> 69.7 us
  between operations: 22.9 us -> 0.69 us
  starting transfers between devices: 12.7 us -> 0 us
  local copies, waits for them, and re-layouts: 12.4 us -> 2.1 us
    another operation x47 -> x0, other arithmetic: 277 us -> none  [the longest x30 159 us: shards(): lower = jnp.linalg.cholesky(outer_self(lower) + outer_self(other_lower))]
    psum x1 -> x0, blocking collectives: 248 us -> none  [shards(): group_gram, group_rhs = lax.psum((gram_part, rhs_part), 'row')]
    psum x1 -> x0, waiting for transfers between devices: 201 us -> none  [shards(): group_gram, group_rhs = lax.psum((gram_part, rhs_part), 'row')]
    dot_general x12 -> x0, matrix products: 69.7 us -> none  [the longest x4 40.7 us: step(): jnp.einsum('fms,fmt->fst', panel, panel, precision=lax.Precision.HIGHEST)]
    pallas_call x0 -> x3, Pallas kernels: none -> 69.7 us  [the longest x1 47.1 us: reduce_all(): pl.pallas_call(functools.partial(reduce_kernel, nx, ny, nz, piece), out_s...]
    ppermute x4 -> x0, waiting for transfers between devices: 19.5 us -> none  [from_partner(): return lax.ppermute(value, axis, pairs)]
    ppermute x4 -> x0, starting transfers between devices: 12.7 us -> none  [from_partner(): return lax.ppermute(value, axis, pairs)]
    another operation x32 -> x0, matrix products: 9 us -> none  [the longest x12 3.75 us: shards(): lower = jnp.linalg.cholesky(outer_self(lower) + outer_self(other_lower))]
  transfers between devices with their start and end apart: 5 -> 0, of which waited for: 3 -> 0; matrix products, arithmetic and copies ran while one was open for 0% -> 0% of each run, Pallas kernels for 0% -> 0%
where the time goes in v1:
time: 72.8 us; the launch traced here: 72.5 us
  Pallas kernels  69.7 us (96%)
  local copies, waits for them, and re-layouts  2.1 us (3%)
    pallas_call x1, Pallas kernels, reduce_all(): pl.pallas_call(functools.partial(reduce_kernel, nx, ny, nz, piece), out_s...  47.1 us
    pallas_call x1, Pallas kernels, solve(): pl.pallas_call(functools.partial(solve_kernel, scale, root, ridge, axis),...  17.8 us
    pallas_call x1, Pallas kernels, panel(): pl.pallas_call(functools.partial(panel_kernel, spacing), out_shape=jax.Sh...  4.84 us
    unnamed x8, local copies, waits for them, and re-layouts  2.1 us

profile of v1, /device:TPU:1, one launch (start us, length us, event | category | flops | bytes accessed | tf_op | source)
XLA Modules:
  0.0 72.5 jit_solution(1038673468137714720)
XLA Ops:
  0.0 0.0 copy-start.3
  0.7 0.0 copy-done.3
  0.7 0.0 copy-start
  0.7 0.7 copy-done
  1.4 0.0 copy-start.1
  1.4 0.7 copy-done.1
  2.1 0.0 copy-start.2
  2.1 0.7 copy-done.2
  2.8 4.8 %panel.1.in_ref = f32[1536,128]{1,0:T(8,128)S(1)} custom-call(s32[1]{0:T(128)S(6)} %copy.6.bin_ref, f32[1,2048]{1,0:T(1,128)S(1)} %copy-done, s32[1,2048]{1,0:T(1,128)S(1)} %copy-done.1, s32[1,2048]{1,0:T(1,128)S(1)} %copy-done.2, s32[1,512]{1,0:T(1,128)S(1)} %bitcast.1), custom_call_target="tpu_custom_call" | custom-call | tf_op jit(solution)/shard_map/panel/pallas_call | solution.py:87
  7.6 47.1 %reduce_all.1.red_ref = f32[1536,128]{1,0:T(8,128)S(1)} custom-call(f32[1536,128]{1,0:T(8,128)S(1)} %panel.1.in_ref), custom_call_target="tpu_custom_call" | custom-call | tf_op jit(solution)/shard_map/reduce_all/pallas_call | solution.py:174
  54.7 17.8 %solve.1 = f32[1,128]{1,0:T(1,128)} custom-call(f32[1536,128]{1,0:T(8,128)S(1)} %reduce_all.1.red_ref), custom_call_target="tpu_custom_call" | custom-call | tf_op jit(solution)/shard_map/solve/pallas_call | solution.py:270
Async XLA Ops:
  0.0 0.7 copy-start.3
  0.7 0.7 copy-start
  1.4 0.7 copy-start.1
  2.1 0.7 copy-start.2

commit v2 on v1

--- a/solution.py
+++ b/solution.py
@@ -34,7 +34,8 @@
     for c in COS[3::-1]: s=s*u+c
     return (s*v) if gain is None else s*(v*gain)
 
-def panel_kernel(spacing, bin_ref, p_ref, cyc_ref, az_ref, src_ref, out_ref, src_scr, mic_scr, hi_scr, lo_scr):
+def panel_gram(loads, spacing, bin_ref, p_ref, cyc_ref, az_ref, src_ref, out_ref, src_scr, mic_scr, hi_scr, lo_scr):
+    loads[0].wait()
     cell=src_ref[...].astype(F32)
     li=jnp.floor((cell+0.5)*0.01); rest=cell-100.0*li
     lj=jnp.floor((rest+0.5)*0.1); ll=rest-10.0*lj
@@ -44,6 +45,8 @@
     rows=[t[0]]*3+[t[1]]*3+[t[2]]*3+[sq]*3+[one]
     sT=jnp.concatenate(rows+[zero]*(128-len(rows)),axis=0)
     src_scr[...]=sT.T.astype(BF)
+    loads[1].wait()
+    loads[2].wait()
     half=spacing*0.5
     polar=(2*cyc_ref[...]+1).astype(F32)*(1.0/16384.0)
     azim=az_ref[...].astype(F32)*(1.0/8192.0)
@@ -57,6 +60,8 @@
     mrows+=[jnp.zeros_like(w)]*(16-len(mrows))
     mic_scr[...]=jnp.concatenate(mrows,axis=0).astype(BF)
     n=p_ref.shape[1]
+    loads[3].wait()
+    loads[4].wait()
     ph,pm=[v.astype(F32) for v in split(p_ref[...],2)]
     hi_scr[S:S+16,:]=jnp.concatenate([ph,pm]+[jnp.zeros_like(ph)]*14,axis=0).astype(BF)
     kc=1.5*(bin_ref[0].astype(F32)+1.0)*float(1/(2*np.pi))
@@ -81,115 +86,157 @@
     out_ref[1280:1288,:]=tail
     out_ref[1288:1536,:]=jnp.zeros((248,128),F32)
 
-def panel(spacing, p, cyc, az, b, src):
-    n=p.shape[1]
-    V=pl.BlockSpec(memory_space=pltpu.VMEM)
-    return pl.pallas_call(functools.partial(panel_kernel,spacing),
-        out_shape=jax.ShapeDtypeStruct((1536,128),F32),
-        in_specs=[pl.BlockSpec(memory_space=pltpu.SMEM),V,V,V,V],out_specs=V,
-        scratch_shapes=[pltpu.VMEM((S,128),BF),pltpu.VMEM((16,n),BF),pltpu.VMEM((S+16,n),BF),pltpu.VMEM((S,n),BF)],
-        name="panel",compiler_params=pltpu.CompilerParams(vmem_limit_bytes=40<<20))(b,p,cyc,az,src.reshape(1,S))
 
 MESH = pl.DeviceIdType.MESH
-
-
-def reduce_kernel(nx, ny, nz, piece, in_ref, out_ref, acc_c, acc_x, acc_y, buf_c, buf_x, buf_y, buf_z,
-                  send_c, recv_c, send_x, recv_x, send_y, recv_y, send_z, recv_z,
-                  gsend_c, grecv_c, gsend_x, grecv_x, gsend_y, grecv_y):
+RING8 = (4, 3, 5, 2, 6, 1, 7)
+
+
+def fit_kernel(dims, spacing, bin_hbm, p_hbm, cyc_hbm, az_hbm, src_hbm, out_ref,
+               bin_ref, p_ref, cyc_ref, az_ref, src_ref, in_sem, src_scr, mic_scr, hi_scr, lo_scr,
+               part, acc_c, acc_x, acc_y, buf_c, buf_x, buf_y, buf_z,
+               send_c, recv_c, send_x, recv_x, send_y, recv_y, send_z, recv_z,
+               gsend_c, grecv_c, gsend_x, grecv_x, gsend_y, grecv_y):
+    nx, ny, nz, piece = dims
     x = lax.axis_index("grp")
     row = lax.axis_index("row")
     c = lax.rem(row, 2)
     y = lax.rem(row // 2, ny)
     z = row // (2 * ny)
-    def at_c(o):
-        return {"row": row + lax.rem(c + o, 2) - c}
+
+    def at_c():
+        return {"row": row + 1 - 2 * c}
+
     def at_x(o):
         return {"grp": lax.rem(x + o, nx)}
+
     def at_y(o):
         return {"row": row + 2 * (lax.rem(y + o, ny) - y)}
+
     def at_z(o):
         return {"row": row + 2 * ny * (lax.rem(z + o, nz) - z)}
-    partners = [at_c(1)] + [at_x(o) for o in range(1, nx)] + [at_y(o) for o in range(1, ny)]
+
+    partners = [at_c()] + [at_x(o) for o in range(1, nx)] + [at_y(o) for o in range(1, ny)]
     partners += [at_z(o) for o in range(1, nz)]
     barrier = pltpu.get_barrier_semaphore()
     for partner in partners:
         pl.semaphore_signal(barrier, inc=1, device_id=partner, device_id_type=MESH)
+
+    loads = []
+    for n, (src, dst) in enumerate([(src_hbm, src_ref), (cyc_hbm, cyc_ref), (az_hbm, az_ref), (bin_hbm, bin_ref),
+                                    (p_hbm, p_ref)]):
+        load = pltpu.make_async_copy(src, dst, in_sem.at[n])
+        load.start()
+        loads.append(load)
+    panel_gram(loads, spacing, bin_ref, p_ref, cyc_ref, az_ref, src_ref, part, src_scr, mic_scr, hi_scr, lo_scr)
     pl.semaphore_wait(barrier, len(partners))
+
+    sends = []
 
     def send(src, dst, ssem, rsem, partner):
         copy = pltpu.make_async_remote_copy(src_ref=src, dst_ref=dst, send_sem=ssem, recv_sem=rsem,
                                             device_id=partner, device_id_type=MESH)
         copy.start()
+        sends.append(copy)
         return copy
 
     def rows(start, count):
         return pl.ds(pl.multiple_of(start, 8), count)
 
-    row_y, row_x, row_c = piece, piece * ny, piece * ny * nx
-    copy = send(in_ref.at[rows((1 - c) * row_c, row_c)], buf_c, send_c, recv_c, at_c(1))
-    copy.wait()
-    acc_c[...] = in_ref[rows(c * row_c, row_c), :] + buf_c[...]
-    copies = [send(acc_c.at[rows(lax.rem(x + o, nx) * row_x, row_x)], buf_x.at[o - 1],
-                   send_x.at[o - 1], recv_x.at[o - 1], at_x(o)) for o in range(1, nx)]
-    for copy in copies:
-        copy.wait()
-    total = acc_c[rows(x * row_x, row_x), :]
-    for o in range(1, nx):
-        total = total + buf_x[o - 1]
-    acc_x[...] = total
-    copies = [send(acc_x.at[rows(lax.rem(y + o, ny) * row_y, row_y)], buf_y.at[o - 1],
-                   send_y.at[o - 1], recv_y.at[o - 1], at_y(o)) for o in range(1, ny)]
-    for copy in copies:
-        copy.wait()
-    total = acc_x[rows(y * row_y, row_y), :]
-    for o in range(1, ny):
-        total = total + buf_y[o - 1]
+    chunk = piece * nx
+
+    def chunk_of(core, yy):
+        return rows((core * ny + yy) * chunk, chunk)
+
+    def piece_of(core, yy, xx):
+        return rows(((core * ny + yy) * nx + xx) * piece, piece)
+
+    far = [o for o in RING8 if o < ny] + [0]
+    targets = [lax.rem(y + o, ny) for o in far]
+    copies_c = [send(part.at[chunk_of(1 - c, t)], buf_c.at[i], send_c.at[i], recv_c.at[i], at_c())
+                for i, t in enumerate(targets)]
+    copies_x = []
+    for i, t in enumerate(targets):
+        copies_c[i].wait_recv()
+        acc_c[i] = part[chunk_of(c, t), :] + buf_c[i]
+        copies_x.append([
+            send(acc_c.at[i, rows(lax.rem(x + o, nx) * piece, piece)], buf_x.at[i, o - 1],
+                 send_x.at[i, o - 1], recv_x.at[i, o - 1], at_x(o)) for o in (2, 1, 3) if o < nx])
+    copies_y = []
+    for i, o in enumerate(far):
+        for copy in copies_x[i]:
+            copy.wait_recv()
+        total = acc_c[i, rows(x * piece, piece), :]
+        for k in range(nx - 1):
+            total = total + buf_x[i, k]
+        acc_x[i] = total
+        if o:
+            copies_y.append(send(acc_x.at[i], buf_y.at[o - 1], send_y.at[o - 1], recv_y.at[o - 1], at_y(o)))
+    for copy in copies_y:
+        copy.wait_recv()
+    for k in range(ny - 1):
+        total = total + buf_y[k]
     acc_y[...] = total
+    copies_z = [send(acc_y, buf_z.at[z], send_z.at[o - 1], recv_z.at[o - 1], at_z(o)) for o in RING8 if o < nz]
     buf_z[z] = total
-    copies = [send(acc_y, buf_z.at[z], send_z.at[o - 1], recv_z.at[o - 1], at_z(o)) for o in range(1, nz)]
-    for copy in copies:
-        copy.wait()
+    for copy in copies_z:
+        copy.wait_recv()
     total = buf_z[0]
-    for o in range(1, nz):
-        total = total + buf_z[o]
-    mine = out_ref.at[rows(c * row_c + x * row_x + y * row_y, row_y)]
+    for k in range(1, nz):
+        total = total + buf_z[k]
+    mine = out_ref.at[piece_of(c, y, x)]
     mine[...] = total
-    copies = [send(mine, mine, gsend_y.at[o - 1], grecv_y.at[o - 1], at_y(o)) for o in range(1, ny)]
-    for copy in copies:
-        copy.wait()
-    mine = out_ref.at[rows(c * row_c + x * row_x, row_x)]
-    copies = [send(mine, mine, gsend_x.at[o - 1], grecv_x.at[o - 1], at_x(o)) for o in range(1, nx)]
-    for copy in copies:
-        copy.wait()
-    mine = out_ref.at[rows(c * row_c, row_c)]
-    send(mine, mine, gsend_c, grecv_c, at_c(1)).wait()
-
-
-def reduce_all(part, nx, ny, nz):
-    piece = part.shape[0] // (2 * nx * ny)
-    vmem = pl.BlockSpec(memory_space=pltpu.VMEM)
+    gather_y = {o: send(mine, mine, gsend_y.at[o - 1], grecv_y.at[o - 1], at_y(o)) for o in RING8 if o < ny}
+    near = [0] + [o for o in RING8[::-1] if o < ny]
+    sources = [lax.rem(y - o + ny, ny) for o in near]
+    gather_x = []
+    for i, o in enumerate(near):
+        if o:
+            gather_y[o].wait_recv()
+        ref = out_ref.at[piece_of(c, sources[i], x)]
+        gather_x.append([send(ref, ref, gsend_x.at[i, k - 1], grecv_x.at[i, k - 1], at_x(k))
+                         for k in (2, 1, 3) if k < nx])
+    gather_c = []
+    for i in range(ny):
+        for copy in gather_x[i]:
+            copy.wait_recv()
+        ref = out_ref.at[chunk_of(c, sources[i])]
+        gather_c.append(send(ref, ref, gsend_c.at[i], grecv_c.at[i], at_c()))
+    for copy in gather_c:
+        copy.wait_recv()
+    for copy in sends:
+        copy.wait_send()
+
+
+def fit(spacing, nx, ny, nz, p, cyc, az, b, src):
+    n = p.shape[1]
+    rows = 1536
+    piece = rows // (2 * nx * ny)
+    anywhere = pl.BlockSpec(memory_space=pltpu.HBM)
     dma = pltpu.SemaphoreType.DMA
-    def pair(count):
-        return [dma((count,)), dma((count,))]
+    v = pltpu.VMEM
+
+    def pair(*shape):
+        return [dma(shape), dma(shape)]
+
     return pl.pallas_call(
-        functools.partial(reduce_kernel, nx, ny, nz, piece),
-        out_shape=jax.ShapeDtypeStruct(part.shape, F32),
-        in_specs=[vmem],
-        out_specs=vmem,
+        functools.partial(fit_kernel, (nx, ny, nz, piece), spacing),
+        out_shape=jax.ShapeDtypeStruct((rows, 128), F32),
+        in_specs=[anywhere] * 5,
+        out_specs=pl.BlockSpec(memory_space=pltpu.VMEM),
         scratch_shapes=[
-            pltpu.VMEM((piece * ny * nx, 128), F32),
-            pltpu.VMEM((piece * ny, 128), F32),
-            pltpu.VMEM((piece, 128), F32),
-            pltpu.VMEM((piece * ny * nx, 128), F32),
-            pltpu.VMEM((nx - 1, piece * ny, 128), F32),
-            pltpu.VMEM((ny - 1, piece, 128), F32),
-            pltpu.VMEM((nz, piece, 128), F32),
-            dma, dma, *pair(nx - 1), *pair(ny - 1), *pair(nz - 1),
-            dma, dma, *pair(nx - 1), *pair(ny - 1),
+            pltpu.SMEM((1,), jnp.int32), v((1, n), F32), v((1, n), jnp.int32), v((1, n), jnp.int32),
+            v((1, S), jnp.int32), dma((5,)),
+            v((S, 128), BF), v((16, n), BF), v((S + 16, n), BF), v((S, n), BF),
+            v((rows, 128), F32),
+            v((ny, piece * nx, 128), F32), v((ny, piece, 128), F32), v((piece, 128), F32),
+            v((ny, piece * nx, 128), F32), v((ny, nx - 1, piece, 128), F32), v((ny - 1, piece, 128), F32),
+            v((nz, piece, 128), F32),
+            *pair(ny), *pair(ny, nx - 1), *pair(ny - 1), *pair(nz - 1),
+            *pair(ny), *pair(ny, nx - 1), *pair(ny - 1),
         ],
-        name="reduce_all",
-        compiler_params=pltpu.CompilerParams(collective_id=0, has_side_effects=True, vmem_limit_bytes=32 << 20),
-    )(part)
+        name="fit",
+        compiler_params=pltpu.CompilerParams(collective_id=0, has_side_effects=True, vmem_limit_bytes=40 << 20),
+    )(b, p, cyc, az, src.reshape(1, S))
 
 TERMS=6; SG=16; PAN=32; LEVEL=0
 def dot(a,b): return jnp.dot(a,b,preferred_element_type=F32)
@@ -212,19 +259,21 @@
         p0=PAN*p
         S=[M[p0+8*q:p0+8*q+8,:] for q in range(nq)]
         for h in range(PAN//SG):
-            B=[[bl(S[q],p0+SG*h+j) for q in range(nq)] for j in range(SG)]
+            B=[jnp.stack([jnp.broadcast_to(S[q][:,c:c+1],(8,128)) for c in range(p0+SG*h,p0+SG*h+SG)]) for q in range(nq)]
             for j in range(SG):
                 row=SG*h+j; qj,rj=divmod(row,8); c=p0+row
-                inv=1.0/bs(B[j][qj],rj)
                 here=lane==c; mine=sub==rj
-                prow=jnp.where(here,1.0,bs(S[qj],rj))*inv
-                for j2 in range(j+1,SG):
-                    raw=bs(B[j2][qj],rj); bp=raw*inv
+                inv=1.0/B[qj][0,rj:rj+1,:]
+                prow=jnp.where(here[:1],1.0,S[qj][rj:rj+1,:])*inv
+                col=[B[q][0] for q in range(nq)]
+                if j<SG-1:
+                    raw=B[qj][1:,rj:rj+1,:]
+                    bp=raw*inv
                     for q in range(nq):
-                        u=B[j2][q]-((B[j][q]*raw)*inv if j2==j+1 else B[j][q]*bp)
-                        B[j2][q]=jnp.where(mine,bp,u) if q==qj else u
+                        nxt=B[q][1:]-col[q]*bp
+                        B[q]=jnp.where(mine,bp,nxt) if q==qj else nxt
                 for q in range(nq):
-                    u=jnp.where(here,0.0,S[q])-B[j][q]*prow
+                    u=jnp.where(here,0.0,S[q])-col[q]*prow
                     S[q]=jnp.where(mine,prow,u) if q==qj else u
         R=jnp.concatenate(S,axis=0)
         pad=[jnp.zeros((PAN,128),F32)]*(128//PAN); pad[p]=R
@@ -234,6 +283,11 @@
     return M
 
 def eliminate(mat):
+    if LEVEL==2:
+        M=mat[0:128,0:128]
+        for k in range(4): M=invert(M)
+        mat[0:128,0:128]=M
+        return
     for k in range(4):
         b=128*k
         Mi=invert(mat[b:b+128,b:b+128])
@@ -279,8 +333,7 @@
     ny = 8
     nz = mesh.shape["row"] // (2 * ny)
     count = pressure.shape[1] * nx * mesh.shape["row"]
-    part = panel(0.08, pressure, mic_cycle, mic_azimuth, bin_index, source_cell)
-    total = reduce_all(part, nx, ny, nz)
+    total = fit(0.08, nx, ny, nz, pressure, mic_cycle, mic_azimuth, bin_index, source_cell)
     return solve(total, 1.0 / count, 1.0 / count**0.5, 0.5, "grp")
 
 

time: 72.8 us -> 64.1 us (0.88)
  Pallas kernels: 69.7 us -> 61 us
    pallas_call x2 -> x1, Pallas kernels: 51.9 us -> 44.2 us  [fit(): pl.pallas_call(functools.partial(fit_kernel, (nx, ny, nz, piece), spacing...]
    pallas_call x1, Pallas kernels: 17.8 us -> 16.8 us  [solve(): pl.pallas_call(functools.partial(solve_kernel, scale, root, ridge, axis),...]
where the time goes in v2:
time: 64.1 us; the launch traced here: 63.8 us
  Pallas kernels  61 us (95%)
  local copies, waits for them, and re-layouts  2.1 us (3%)
  between operations  0.68 us (1%)
    pallas_call x1, Pallas kernels, fit(): pl.pallas_call(functools.partial(fit_kernel, (nx, ny, nz, piece), spacing...  44.2 us
    pallas_call x1, Pallas kernels, solve(): pl.pallas_call(functools.partial(solve_kernel, scale, root, ridge, axis),...  16.8 us
    unnamed x8, local copies, waits for them, and re-layouts  2.1 us

profile of v2, /device:TPU:1, one launch (start us, length us, event | category | flops | bytes accessed | tf_op | source)
XLA Modules:
  0.0 63.8 jit_solution(6417071080959468396)
XLA Ops:
  0.0 0.0 copy-start.3
  0.7 0.0 copy-done.3
  0.7 0.0 copy-start
  0.7 0.7 %copy-done = f32[1,2048]{1,0:T(1,128)S(1)} copy-done((f32[1,2048]{1,0:T(1,128)S(1)}, f32[1,2048]{1,0:T(1,128)}, u32[]{:S(2)}) %copy-start) | copy-done | bytes 8216
  1.4 0.0 copy-start.1
  1.4 0.7 %copy-done.1 = s32[1,2048]{1,0:T(1,128)S(1)} copy-done((s32[1,2048]{1,0:T(1,128)S(1)}, s32[1,2048]{1,0:T(1,128)}, u32[]{:S(2)}) %copy-start.1) | copy-done | bytes 8216
  2.1 0.0 copy-start.2
  2.1 0.7 %copy-done.2 = s32[1,2048]{1,0:T(1,128)S(1)} copy-done((s32[1,2048]{1,0:T(1,128)S(1)}, s32[1,2048]{1,0:T(1,128)}, u32[]{:S(2)}) %copy-start.2) | copy-done | bytes 8216
  2.8 44.2 %fit.1.red_ref = f32[1536,128]{1,0:T(8,128)S(1)} custom-call(s32[1]{0:T(128)S(6)} %copy.6.bin_hbm, f32[1,2048]{1,0:T(1,128)S(1)} %copy-done, s32[1,2048]{1,0:T(1,128)S(1)} %copy-done.1, s32[1,2048]{1,0:T(1,128)S(1)} %copy-done.2, s32[1,512]{1,0:T(1,128)S(1)} %bitcast.1), custom_call_target="tpu_custom_call" | custom-call | tf_op jit(solution)/shard_map/fit/pallas_call | solution.py:221
  47.0 16.8 %solve.1 = f32[1,128]{1,0:T(1,128)} custom-call(f32[1536,128]{1,0:T(8,128)S(1)} %fit.1.red_ref), custom_call_target="tpu_custom_call" | custom-call | tf_op jit(solution)/shard_map/solve/pallas_call | solution.py:324
Async XLA Ops:
  0.0 0.7 %copy-start.3 = (s32[512]{0:T(512)S(1)}, s32[512]{0:T(512)}, u32[]{:S(2)}) copy-start(s32[512]{0:T(512)} %param.9) | copy-start | bytes 6148
  0.7 0.7 %copy-start = (f32[1,2048]{1,0:T(1,128)S(1)}, f32[1,2048]{1,0:T(1,128)}, u32[]{:S(2)}) copy-start(f32[1,2048]{1,0:T(1,128)} %p_hbm.1) | copy-start | bytes 24580
  1.4 0.7 %copy-start.1 = (s32[1,2048]{1,0:T(1,128)S(1)}, s32[1,2048]{1,0:T(1,128)}, u32[]{:S(2)}) copy-start(s32[1,2048]{1,0:T(1,128)} %cyc_hbm.1) | copy-start | bytes 24580
  2.1 0.7 %copy-start.2 = (s32[1,2048]{1,0:T(1,128)S(1)}, s32[1,2048]{1,0:T(1,128)}, u32[]{:S(2)}) copy-start(s32[1,2048]{1,0:T(1,128)} %az_hbm.1) | copy-start | bytes 24580

commit v3 on v2

--- a/solution.py
+++ b/solution.py
@@ -17,7 +17,7 @@
 
 NT=(((1,),(1,)),((),()))
 CHUNK=256
-COS=[float(v) for v in (6.283185307179586,-41.34170224039975,81.60524927607504,-76.70585975306136,42.05869394489765)]
+SINE=(6.283185160089467, -41.341655031414675, 81.60100407316348, -76.54978229140988, 39.5367060495799)
 MAGIC=12582912.0
 
 def split(v,n):
@@ -30,8 +30,8 @@
     y=t-((t+MAGIC)-MAGIC)
     v=0.25-jnp.abs(y)
     u=v*v
-    s=COS[4]
-    for c in COS[3::-1]: s=s*u+c
+    s=SINE[4]
+    for c in SINE[3::-1]: s=s*u+c
     return (s*v) if gain is None else s*(v*gain)
 
 def panel_gram(loads, spacing, bin_ref, p_ref, cyc_ref, az_ref, src_ref, out_ref, src_scr, mic_scr, hi_scr, lo_scr):
@@ -87,13 +87,105 @@
     out_ref[1288:1536,:]=jnp.zeros((248,128),F32)
 
 
+TERMS=6; INNER=3; SG=16
+def dot(a,b): return jnp.dot(a,b,preferred_element_type=F32)
+def mm(a,b):
+    if TERMS==3:
+        ah,am=split(a,2); bh,bm=split(b,2)
+        return dot(jnp.concatenate([ah,am],1),jnp.concatenate([bh,bh],0))+dot(ah,bm)
+    if TERMS==6:
+        ah,am,al=split(a,3); bh,bm,bl_=split(b,3)
+        ahm=jnp.concatenate([ah,am],1)
+        return (dot(jnp.concatenate([ah,al],1),jnp.concatenate([bl_,bh],0))+dot(ahm,jnp.concatenate([bm,bm],0)))+dot(ahm,jnp.concatenate([bh,bh],0))
+    if TERMS==1:
+        return dot(a.astype(BF),b.astype(BF))
+    return jnp.dot(a,b,precision=lax.Precision.HIGHEST,preferred_element_type=F32)
+
+def bl(v,c): return jnp.broadcast_to(v[:,c:c+1],(8,128))
+def bs(v,r): return jnp.broadcast_to(v[r:r+1,:],(8,128))
+
+def mm_inner(a,b):
+    if INNER==3:
+        ah,am=split(a,2); bh,bm=split(b,2)
+        return dot(jnp.concatenate([ah,am],1),jnp.concatenate([bh,bh],0))+dot(ah,bm)
+    if INNER==6:
+        ah,am,al=split(a,3); bh,bm,bl_=split(b,3)
+        ahm=jnp.concatenate([ah,am],1)
+        return (dot(jnp.concatenate([ah,al],1),jnp.concatenate([bl_,bh],0))+dot(ahm,jnp.concatenate([bm,bm],0)))+dot(ahm,jnp.concatenate([bh,bh],0))
+    return jnp.dot(a,b,precision=lax.Precision.HIGHEST,preferred_element_type=F32)
+
+def sweep(S, first, c0, lane, sub):
+    nq=len(S)
+    B=[jnp.stack([jnp.broadcast_to(S[q][:,c:c+1],(8,128)) for c in range(c0,c0+SG)]) for q in range(nq)]
+    piv=(lane>=c0)&(lane<c0+SG)
+    for q in range(nq):
+        fill=jnp.where(lane-c0==sub+(8*q-first),1.0,0.0) if first<=8*q<first+SG else 0.0
+        S[q]=jnp.where(piv,fill,S[q])
+    scale=[None]*nq
+    for j in range(SG):
+        qj,rj=divmod(first+j,8)
+        mine=sub==rj
+        inv=1.0/jnp.broadcast_to(B[qj][0,rj:rj+1,:],(8,128))
+        rawS=S[qj][rj:rj+1,:]
+        g=[(jnp.where(mine,0.0,B[q][0]) if q==qj else B[q][0])*inv for q in range(nq)]
+        scale[qj]=inv if scale[qj] is None else jnp.where(sub>=rj,inv,scale[qj])
+        if j<SG-1:
+            raw=B[qj][1:,rj:rj+1,:]
+            B=[B[q][1:]-g[q]*raw for q in range(nq)]
+        S=[S[q]-g[q]*rawS for q in range(nq)]
+    return [S[q] if scale[q] is None else S[q]*scale[q] for q in range(nq)]
+
+def invert(M):
+    lane=lax.broadcasted_iota(jnp.int32,(8,128),1); sub=lax.broadcasted_iota(jnp.int32,(8,128),0)
+    biglane=lax.broadcasted_iota(jnp.int32,(128,128),1)
+    def put(rows, start, into):
+        return jnp.concatenate([x for x in [into[:start],rows,into[start+rows.shape[0]:]] if x.shape[0]],axis=0)
+    zero=jnp.zeros((128,128),F32)
+    ahead=[M[8*q:8*q+8,:] for q in range(2)]
+    for g in range(8):
+        p0=16*g
+        S=ahead+([M[p0+16+8*q:p0+24+8*q,:] for q in range(2)] if g<7 else [])
+        S=sweep(S,0,p0,lane,sub)
+        ahead=S[2:]
+        R=jnp.concatenate(S[:2],axis=0)
+        M=jnp.where((biglane>=p0)&(biglane<p0+16),0.0,M)-mm_inner(M,put(R,p0,zero))
+        M=put(R,p0,M)
+    return M
+
+def eliminate(mat):
+    for k in range(4):
+        b=128*k
+        Mi=invert(mat[b:b+128,b:b+128])
+        R=mm(Mi,mat[b:b+128,b+128:])
+        order=[(k+1+t)%4 for t in range(3)]
+        if k<3:
+            o=k+1
+            mat[128*o:128*o+128,128*o:128*o+128]-=mm(mat[128*o:128*o+128,b:b+128],R[:,:128])
+            mat[128*o:128*o+128,128*o+128:]-=mm(mat[128*o:128*o+128,b:b+128],R[:,128:])
+            order=order[1:]
+        for o in order:
+            mat[128*o:128*o+128,b+128:]-=mm(mat[128*o:128*o+128,b:b+128],R)
+        mat[b:b+128,b+128:]=R
+
+def assemble(red_ref, mat, scale, root, ridge):
+    r=lax.broadcasted_iota(jnp.int32,(128,128),0); c=lax.broadcasted_iota(jnp.int32,(128,128),1)
+    for n,(i,j) in enumerate(PAIRS):
+        b=red_ref[128*n:128*n+128,:]*scale
+        if i==j: b=b+jnp.where(r==c,ridge,0.0)
+        mat[128*i:128*i+128,128*j:128*j+128]=b
+        if i!=j: mat[128*j:128*j+128,128*i:128*i+128]=b.T
+    for i in range(4):
+        row=red_ref[1280+i:1281+i,:]*root
+        mat[128*i:128*i+128,512:640]=jnp.broadcast_to(row,(128,128)).T
+
+
 MESH = pl.DeviceIdType.MESH
 RING8 = (4, 3, 5, 2, 6, 1, 7)
 
 
-def fit_kernel(dims, spacing, bin_hbm, p_hbm, cyc_hbm, az_hbm, src_hbm, out_ref,
+def fit_kernel(dims, consts, bin_hbm, p_hbm, cyc_hbm, az_hbm, src_hbm, out_ref,
                bin_ref, p_ref, cyc_ref, az_ref, src_ref, in_sem, src_scr, mic_scr, hi_scr, lo_scr,
-               part, acc_c, acc_x, acc_y, buf_c, buf_x, buf_y, buf_z,
+               part, full, mat, acc_c, acc_x, acc_y, buf_c, buf_x, buf_y, buf_z,
                send_c, recv_c, send_x, recv_x, send_y, recv_y, send_z, recv_z,
                gsend_c, grecv_c, gsend_x, grecv_x, gsend_y, grecv_y):
     nx, ny, nz, piece = dims
@@ -127,6 +219,7 @@
         load = pltpu.make_async_copy(src, dst, in_sem.at[n])
         load.start()
         loads.append(load)
+    scale, root, ridge, spacing = consts
     panel_gram(loads, spacing, bin_ref, p_ref, cyc_ref, az_ref, src_ref, part, src_scr, mic_scr, hi_scr, lo_scr)
     pl.semaphore_wait(barrier, len(partners))
 
@@ -183,7 +276,7 @@
     total = buf_z[0]
     for k in range(1, nz):
         total = total + buf_z[k]
-    mine = out_ref.at[piece_of(c, y, x)]
+    mine = full.at[piece_of(c, y, x)]
     mine[...] = total
     gather_y = {o: send(mine, mine, gsend_y.at[o - 1], grecv_y.at[o - 1], at_y(o)) for o in RING8 if o < ny}
     near = [0] + [o for o in RING8[::-1] if o < ny]
@@ -192,26 +285,30 @@
     for i, o in enumerate(near):
         if o:
             gather_y[o].wait_recv()
-        ref = out_ref.at[piece_of(c, sources[i], x)]
+        ref = full.at[piece_of(c, sources[i], x)]
         gather_x.append([send(ref, ref, gsend_x.at[i, k - 1], grecv_x.at[i, k - 1], at_x(k))
                          for k in (2, 1, 3) if k < nx])
     gather_c = []
     for i in range(ny):
         for copy in gather_x[i]:
             copy.wait_recv()
-        ref = out_ref.at[chunk_of(c, sources[i])]
+        ref = full.at[chunk_of(c, sources[i])]
         gather_c.append(send(ref, ref, gsend_c.at[i], grecv_c.at[i], at_c()))
     for copy in gather_c:
         copy.wait_recv()
+    assemble(full, mat, scale, root, ridge)
+    eliminate(mat)
+    block = mat[pl.ds(pl.multiple_of(x * 128, 128), 128), 512:640]
+    out_ref[...] = block.T[0:1, :]
     for copy in sends:
         copy.wait_send()
 
 
-def fit(spacing, nx, ny, nz, p, cyc, az, b, src):
+def fit(consts, nx, ny, nz, p, cyc, az, b, src):
     n = p.shape[1]
     rows = 1536
     piece = rows // (2 * nx * ny)
-    anywhere = pl.BlockSpec(memory_space=pltpu.HBM)
+    anywhere = pl.BlockSpec(memory_space=pl.ANY)
     dma = pltpu.SemaphoreType.DMA
     v = pltpu.VMEM
 
@@ -219,15 +316,15 @@
         return [dma(shape), dma(shape)]
 
     return pl.pallas_call(
-        functools.partial(fit_kernel, (nx, ny, nz, piece), spacing),
-        out_shape=jax.ShapeDtypeStruct((rows, 128), F32),
+        functools.partial(fit_kernel, (nx, ny, nz, piece), consts),
+        out_shape=jax.ShapeDtypeStruct((1, 128), F32),
         in_specs=[anywhere] * 5,
         out_specs=pl.BlockSpec(memory_space=pltpu.VMEM),
         scratch_shapes=[
             pltpu.SMEM((1,), jnp.int32), v((1, n), F32), v((1, n), jnp.int32), v((1, n), jnp.int32),
             v((1, S), jnp.int32), dma((5,)),
             v((S, 128), BF), v((16, n), BF), v((S + 16, n), BF), v((S, n), BF),
-            v((rows, 128), F32),
+            v((rows, 128), F32), v((rows, 128), F32), v((512, 640), F32),
             v((ny, piece * nx, 128), F32), v((ny, piece, 128), F32), v((piece, 128), F32),
             v((ny, piece * nx, 128), F32), v((ny, nx - 1, piece, 128), F32), v((ny - 1, piece, 128), F32),
             v((nz, piece, 128), F32),
@@ -235,97 +332,8 @@
             *pair(ny), *pair(ny, nx - 1), *pair(ny - 1),
         ],
         name="fit",
-        compiler_params=pltpu.CompilerParams(collective_id=0, has_side_effects=True, vmem_limit_bytes=40 << 20),
+        compiler_params=pltpu.CompilerParams(collective_id=0, has_side_effects=True, vmem_limit_bytes=56 << 20),
     )(b, p, cyc, az, src.reshape(1, S))
-
-TERMS=6; SG=16; PAN=32; LEVEL=0
-def dot(a,b): return jnp.dot(a,b,preferred_element_type=F32)
-def mm(a,b):
-    if TERMS==3:
-        ah,am=split(a,2); bh,bm=split(b,2)
-        return dot(jnp.concatenate([ah,am],1),jnp.concatenate([bh,bh],0))+dot(ah,bm)
-    if TERMS==1:
-        return dot(a.astype(BF),b.astype(BF))
-    return jnp.dot(a,b,precision=lax.Precision.HIGHEST,preferred_element_type=F32)
-
-def bl(v,c): return jnp.broadcast_to(v[:,c:c+1],(8,128))
-def bs(v,r): return jnp.broadcast_to(v[r:r+1,:],(8,128))
-
-def invert(M):
-    lane=lax.broadcasted_iota(jnp.int32,(8,128),1); sub=lax.broadcasted_iota(jnp.int32,(8,128),0)
-    biglane=lax.broadcasted_iota(jnp.int32,(128,128),1)
-    nq=PAN//8
-    for p in range(128//PAN):
-        p0=PAN*p
-        S=[M[p0+8*q:p0+8*q+8,:] for q in range(nq)]
-        for h in range(PAN//SG):
-            B=[jnp.stack([jnp.broadcast_to(S[q][:,c:c+1],(8,128)) for c in range(p0+SG*h,p0+SG*h+SG)]) for q in range(nq)]
-            for j in range(SG):
-                row=SG*h+j; qj,rj=divmod(row,8); c=p0+row
-                here=lane==c; mine=sub==rj
-                inv=1.0/B[qj][0,rj:rj+1,:]
-                prow=jnp.where(here[:1],1.0,S[qj][rj:rj+1,:])*inv
-                col=[B[q][0] for q in range(nq)]
-                if j<SG-1:
-                    raw=B[qj][1:,rj:rj+1,:]
-                    bp=raw*inv
-                    for q in range(nq):
-                        nxt=B[q][1:]-col[q]*bp
-                        B[q]=jnp.where(mine,bp,nxt) if q==qj else nxt
-                for q in range(nq):
-                    u=jnp.where(here,0.0,S[q])-col[q]*prow
-                    S[q]=jnp.where(mine,prow,u) if q==qj else u
-        R=jnp.concatenate(S,axis=0)
-        pad=[jnp.zeros((PAN,128),F32)]*(128//PAN); pad[p]=R
-        Rp=jnp.concatenate(pad,axis=0)
-        upd=jnp.where((biglane>=p0)&(biglane<p0+PAN),0.0,M)-mm(M,Rp)
-        M=jnp.concatenate([x for x in [upd[:p0],R,upd[p0+PAN:]] if x.shape[0]],axis=0)
-    return M
-
-def eliminate(mat):
-    if LEVEL==2:
-        M=mat[0:128,0:128]
-        for k in range(4): M=invert(M)
-        mat[0:128,0:128]=M
-        return
-    for k in range(4):
-        b=128*k
-        Mi=invert(mat[b:b+128,b:b+128])
-        R=mm(Mi,mat[b:b+128,b+128:])
-        order=[(k+1+t)%4 for t in range(3)]
-        if k<3:
-            o=k+1
-            mat[128*o:128*o+128,128*o:128*o+128]-=mm(mat[128*o:128*o+128,b:b+128],R[:,:128])
-            mat[128*o:128*o+128,128*o+128:]-=mm(mat[128*o:128*o+128,b:b+128],R[:,128:])
-            order=order[1:]
-        for o in order:
-            mat[128*o:128*o+128,b+128:]-=mm(mat[128*o:128*o+128,b:b+128],R)
-        mat[b:b+128,b+128:]=R
-
-def assemble(red_ref, mat, scale, root, ridge):
-    r=lax.broadcasted_iota(jnp.int32,(128,128),0); c=lax.broadcasted_iota(jnp.int32,(128,128),1)
-    for n,(i,j) in enumerate(PAIRS):
-        b=red_ref[128*n:128*n+128,:]*scale
-        if i==j: b=b+jnp.where(r==c,ridge,0.0)
-        mat[128*i:128*i+128,128*j:128*j+128]=b
-        if i!=j: mat[128*j:128*j+128,128*i:128*i+128]=b.T
-    for i in range(4):
-        row=red_ref[1280+i:1281+i,:]*root
-        mat[128*i:128*i+128,512:640]=jnp.broadcast_to(row,(128,128)).T
-
-def solve_kernel(scale, root, ridge, axis, red_ref, out_ref, mat):
-    assemble(red_ref, mat, scale, root, ridge)
-    if LEVEL!=1: eliminate(mat)
-    me=lax.axis_index(axis) if axis else 1
-    blk=mat[pl.ds(pl.multiple_of(me*128,128),128),512:640]
-    out_ref[...]=blk.T[0:1,:]
-
-def solve(red, scale, root, ridge, axis):
-    return pl.pallas_call(functools.partial(solve_kernel,scale,root,ridge,axis),
-        out_shape=jax.ShapeDtypeStruct((1,128),jnp.float32),
-        in_specs=[pl.BlockSpec(memory_space=pltpu.VMEM)],out_specs=pl.BlockSpec(memory_space=pltpu.VMEM),
-        scratch_shapes=[pltpu.VMEM((512,640),jnp.float32)],name="solve",
-        compiler_params=pltpu.CompilerParams(vmem_limit_bytes=32<<20))(red)
 
 
 def shards(mesh, pressure, mic_cycle, mic_azimuth, bin_index, source_cell):
@@ -333,8 +341,8 @@
     ny = 8
     nz = mesh.shape["row"] // (2 * ny)
     count = pressure.shape[1] * nx * mesh.shape["row"]
-    total = fit(0.08, nx, ny, nz, pressure, mic_cycle, mic_azimuth, bin_index, source_cell)
-    return solve(total, 1.0 / count, 1.0 / count**0.5, 0.5, "grp")
+    consts = (1.0 / count, 1.0 / count**0.5, 0.5, 0.08)
+    return fit(consts, nx, ny, nz, pressure, mic_cycle, mic_azimuth, bin_index, source_cell)
 
 
 def solution(mesh):

time: 64.1 us -> 59.5 us (0.928)
  Pallas kernels: 61 us -> 57.5 us
  local copies, waits for them, and re-layouts: 2.1 us -> 1.19 us
    pallas_call x2 -> x1, Pallas kernels: 61 us -> 57.5 us  [fit(): pl.pallas_call(functools.partial(fit_kernel, (nx, ny, nz, piece), consts)...]
    unnamed x8 -> x1, local copies, waits for them, and re-layouts: 2.1 us -> 1.19 us
where the time goes in v3:
time: 59.5 us; the launch traced here: 59.4 us
  Pallas kernels  57.5 us (97%)
  local copies, waits for them, and re-layouts  1.19 us (2%)
  between operations  0.66 us (1%)
    pallas_call x1, Pallas kernels, fit(): pl.pallas_call(functools.partial(fit_kernel, (nx, ny, nz, piece), consts)...  57.5 us
    unnamed x1, local copies, waits for them, and re-layouts  1.19 us

profile of v3, /device:TPU:1, one launch (start us, length us, event | category | flops | bytes accessed | tf_op | source)
XLA Modules:
  0.0 59.4 jit_solution(13213973737833079191)
XLA Ops:
  0.7 57.5 %fit.1 = f32[1,128]{1,0:T(1,128)} custom-call(s32[1]{0:T(128)S(6)} %copy.7.bin_hbm, f32[1,2048]{1,0:T(1,128)} %p_hbm.1, s32[1,2048]{1,0:T(1,128)} %cyc_hbm.1, s32[1,2048]{1,0:T(1,128)} %az_hbm.1, s32[1,512]{1,0:T(1,128)} %bitcast.1), custom_call_target="tpu_custom_call" | custom-call | tf_op jit(solution)/shard_map/fit/pallas_call | solution.py:318
  58.2 1.2 %copy.8 = f32[1,128]{1,0:T(1,128)} copy(f32[1,128]{1,0:T(1,128)} %fit.1) | data formatting | bytes 1024

commit v4 on v3

--- a/solution.py
+++ b/solution.py
@@ -16,7 +16,7 @@
 PAIRS = [(i, j) for i in range(4) for j in range(i, 4)]
 
 NT=(((1,),(1,)),((),()))
-CHUNK=256
+CHUNK=512
 SINE=(6.283185160089467, -41.341655031414675, 81.60100407316348, -76.54978229140988, 39.5367060495799)
 MAGIC=12582912.0
 
@@ -34,58 +34,88 @@
     for c in SINE[3::-1]: s=s*u+c
     return (s*v) if gain is None else s*(v*gain)
 
+def bf16_parts(value, n):
+    parts = []
+    for _ in range(n):
+        part = float(np.float32(value).astype(jnp.bfloat16))
+        parts.append(part)
+        value -= part
+    return parts
+
+
+UNIT=bf16_parts((1.5/(2*np.pi))**2, 3)
+HALF=256
+
+
+def order_of(bin_ref):
+    order = bin_ref[0].astype(F32) + 1.0
+    return order * order
+
+
 def panel_gram(loads, spacing, bin_ref, p_ref, cyc_ref, az_ref, src_ref, out_ref, src_scr, mic_scr, hi_scr, lo_scr):
     loads[0].wait()
+    loads[3].wait()
     cell=src_ref[...].astype(F32)
     li=jnp.floor((cell+0.5)*0.01); rest=cell-100.0*li
     lj=jnp.floor((rest+0.5)*0.1); ll=rest-10.0*lj
     t=[2.0*v-9.0 for v in (li,lj,ll)]
     sq=t[0]*t[0]+t[1]*t[1]+t[2]*t[2]
     one=jnp.ones_like(sq); zero=jnp.zeros_like(sq)
-    rows=[t[0]]*3+[t[1]]*3+[t[2]]*3+[sq]*3+[one]
+    sq_order=one*(order_of(bin_ref))
+    rows=[t[0]]*3+[t[1]]*3+[t[2]]*3+[sq]*3+[sq_order]*3
     sT=jnp.concatenate(rows+[zero]*(128-len(rows)),axis=0)
     src_scr[...]=sT.T.astype(BF)
     loads[1].wait()
     loads[2].wait()
+    order=bin_ref[0].astype(F32)+1.0
+    turns=(order*order)*float((1.5/(2*np.pi))**2)
     half=spacing*0.5
     polar=(2*cyc_ref[...]+1).astype(F32)*(1.0/16384.0)
     azim=az_ref[...].astype(F32)*(1.0/8192.0)
     sp=cos_turns(polar-0.25); cp=cos_turns(polar)
     mic=[sp*cos_turns(azim), sp*cos_turns(azim-0.25), cp]
     mrows=[]
-    for m in mic: mrows+=split(m*(-2.0*half),3)
-    w=jnp.full(mic[0].shape,half*half,F32)
-    mrows+=split(w,3)+[jnp.ones_like(w).astype(BF)]
+    for m in mic: mrows+=split(m*(turns*(-2.0*half)),3)
+    w=jnp.full(mic[0].shape,half*half,F32)*turns
+    mrows+=split(w,3)+[jnp.full(w.shape,v,BF) for v in UNIT]
     mrows=[m.astype(F32) for m in mrows]
     mrows+=[jnp.zeros_like(w)]*(16-len(mrows))
     mic_scr[...]=jnp.concatenate(mrows,axis=0).astype(BF)
     n=p_ref.shape[1]
-    loads[3].wait()
     loads[4].wait()
     ph,pm=[v.astype(F32) for v in split(p_ref[...],2)]
-    hi_scr[S:S+16,:]=jnp.concatenate([ph,pm]+[jnp.zeros_like(ph)]*14,axis=0).astype(BF)
-    kc=1.5*(bin_ref[0].astype(F32)+1.0)*float(1/(2*np.pi))
-    for c in range(n//CHUNK):
-        cols=slice(c*CHUNK,(c+1)*CHUNK)
-        d2=jnp.dot(src_scr[:,:16],mic_scr[:,cols],preferred_element_type=F32)
-        r=lax.rsqrt(d2)
-        val=cos_turns((d2*r)*kc, r)
-        h=val.astype(BF)
-        hi_scr[0:S,cols]=h
-        lo_scr[:,cols]=(val-h.astype(F32)).astype(BF)
-    H=lax.dot_general(hi_scr[...],hi_scr[0:S,:],NT,preferred_element_type=F32)
-    L=lax.dot_general(hi_scr[...],lo_scr[...],NT,preferred_element_type=F32)
-    nblk=0
-    for i in range(4):
-        for j in range(i,4):
-            a=slice(128*i,128*i+128); b=slice(128*j,128*j+128)
-            out_ref[128*nblk:128*nblk+128,:]=H[a,b]+L[a,b]+L[b,a].T
-            nblk+=1
-    r=(H[S:S+1]+L[S:S+1])+(H[S+1:S+2]+L[S+1:S+2])
-    tail=jnp.concatenate([r[:,128*i:128*i+128] for i in range(4)]+[jnp.zeros((4,128),F32)],axis=0)
-    out_ref[1280:1288,:]=tail
+    hi_scr[HALF:HALF+16,:]=jnp.concatenate([ph,pm]+[jnp.zeros_like(ph)]*14,axis=0).astype(BF)
+    for lo in range(0, S, HALF):
+        for c in range(n//CHUNK):
+            cols=slice(c*CHUNK,(c+1)*CHUNK)
+            t2=jnp.dot(src_scr[lo:lo+HALF,:16],mic_scr[:,cols],preferred_element_type=F32)
+            r=lax.rsqrt(t2)
+            val=cos_turns(t2*r, r)
+            h=val.astype(BF)
+            hi_scr[lo+(16 if lo else 0):lo+(16 if lo else 0)+HALF,cols]=h
+            lo_scr[lo:lo+HALF,cols]=(val-h.astype(F32)).astype(BF)
+    unit=1.5*(bin_ref[0].astype(F32)+1.0)*float(1/(2*np.pi))
+    gain=unit*unit
+    def product(a, b):
+        return lax.dot_general(a, b, NT, preferred_element_type=F32)
+    R0=HALF+16
+    H1=product(hi_scr[0:R0],hi_scr[0:HALF]); L1=product(hi_scr[...],lo_scr[0:HALF])
+    H2=product(hi_scr[...],hi_scr[R0:]); L2=product(hi_scr[...],lo_scr[HALF:S])
+    def at(i):
+        return 128*i+(16 if i>=2 else 0)
+    def hblk(i,j):
+        m=H1 if j<2 else H2
+        return m[at(i):at(i)+128,128*(j%2):128*(j%2)+128]
+    def lblk(i,j):
+        m=L1 if j<2 else L2
+        return m[at(i):at(i)+128,128*(j%2):128*(j%2)+128]
+    for k,(i,j) in enumerate(PAIRS):
+        out_ref[128*k:128*k+128,:]=((hblk(i,j)+lblk(i,j))+lblk(j,i).T)*gain
+    r1=(H1[HALF:HALF+1]+L1[HALF:HALF+1])+(H1[HALF+1:HALF+2]+L1[HALF+1:HALF+2])
+    r2=(H2[HALF:HALF+1]+L2[HALF:HALF+1])+(H2[HALF+1:HALF+2]+L2[HALF+1:HALF+2])
+    tail=jnp.concatenate([r1[:,:128],r1[:,128:],r2[:,:128],r2[:,128:],jnp.zeros((4,128),F32)],axis=0)
+    out_ref[1280:1288,:]=tail*unit
     out_ref[1288:1536,:]=jnp.zeros((248,128),F32)
-
 
 TERMS=6; INNER=3; SG=16
 def dot(a,b): return jnp.dot(a,b,preferred_element_type=F32)
@@ -135,7 +165,7 @@
         S=[S[q]-g[q]*rawS for q in range(nq)]
     return [S[q] if scale[q] is None else S[q]*scale[q] for q in range(nq)]
 
-def invert(M):
+def invert(M, between=None):
     lane=lax.broadcasted_iota(jnp.int32,(8,128),1); sub=lax.broadcasted_iota(jnp.int32,(8,128),0)
     biglane=lax.broadcasted_iota(jnp.int32,(128,128),1)
     def put(rows, start, into):
@@ -144,6 +174,8 @@
     ahead=[M[8*q:8*q+8,:] for q in range(2)]
     for g in range(8):
         p0=16*g
+        if between is not None:
+            between(g)
         S=ahead+([M[p0+16+8*q:p0+24+8*q,:] for q in range(2)] if g<7 else [])
         S=sweep(S,0,p0,lane,sub)
         ahead=S[2:]
@@ -152,10 +184,12 @@
         M=put(R,p0,M)
     return M
 
-def eliminate(mat):
+def eliminate(mat, between, rest):
     for k in range(4):
         b=128*k
-        Mi=invert(mat[b:b+128,b:b+128])
+        Mi=invert(mat[b:b+128,b:b+128], between if k==0 else None)
+        if k==0:
+            rest()
         R=mm(Mi,mat[b:b+128,b+128:])
         order=[(k+1+t)%4 for t in range(3)]
         if k<3:
@@ -167,27 +201,30 @@
             mat[128*o:128*o+128,b+128:]-=mm(mat[128*o:128*o+128,b:b+128],R)
         mat[b:b+128,b+128:]=R
 
-def assemble(red_ref, mat, scale, root, ridge):
+def assemble(red_ref, mat, scale, root, ridge, start, stop):
     r=lax.broadcasted_iota(jnp.int32,(128,128),0); c=lax.broadcasted_iota(jnp.int32,(128,128),1)
-    for n,(i,j) in enumerate(PAIRS):
+    for n in range(start,stop):
+        i,j=PAIRS[n]
         b=red_ref[128*n:128*n+128,:]*scale
         if i==j: b=b+jnp.where(r==c,ridge,0.0)
         mat[128*i:128*i+128,128*j:128*j+128]=b
         if i!=j: mat[128*j:128*j+128,128*i:128*i+128]=b.T
-    for i in range(4):
-        row=red_ref[1280+i:1281+i,:]*root
-        mat[128*i:128*i+128,512:640]=jnp.broadcast_to(row,(128,128)).T
-
+    if stop==len(PAIRS):
+        for i in range(4):
+            row=red_ref[1280+i:1281+i,:]*root
+            mat[128*i:128*i+128,512:640]=jnp.broadcast_to(row,(128,128)).T
 
 MESH = pl.DeviceIdType.MESH
 RING8 = (4, 3, 5, 2, 6, 1, 7)
+OUTWARD = tuple((i,) for i in range(8))
+HOMEWARD = ((0, 1), (2, 3, 4, 5, 6, 7))
+MIDWAY = 3
 
 
 def fit_kernel(dims, consts, bin_hbm, p_hbm, cyc_hbm, az_hbm, src_hbm, out_ref,
                bin_ref, p_ref, cyc_ref, az_ref, src_ref, in_sem, src_scr, mic_scr, hi_scr, lo_scr,
                part, full, mat, acc_c, acc_x, acc_y, buf_c, buf_x, buf_y, buf_z,
-               send_c, recv_c, send_x, recv_x, send_y, recv_y, send_z, recv_z,
-               gsend_c, grecv_c, gsend_x, grecv_x, gsend_y, grecv_y):
+               send_sem, recv_c, recv_x, recv_y, recv_z, grecv_y, grecv_x, grecv_c):
     nx, ny, nz, piece = dims
     x = lax.axis_index("grp")
     row = lax.axis_index("row")
@@ -223,18 +260,21 @@
     panel_gram(loads, spacing, bin_ref, p_ref, cyc_ref, az_ref, src_ref, part, src_scr, mic_scr, hi_scr, lo_scr)
     pl.semaphore_wait(barrier, len(partners))
 
-    sends = []
-
     def send(src, dst, ssem, rsem, partner):
-        copy = pltpu.make_async_remote_copy(src_ref=src, dst_ref=dst, send_sem=ssem, recv_sem=rsem,
-                                            device_id=partner, device_id_type=MESH)
-        copy.start()
-        sends.append(copy)
-        return copy
+        pltpu.make_async_remote_copy(src_ref=src, dst_ref=dst, send_sem=ssem, recv_sem=rsem,
+                                     device_id=partner, device_id_type=MESH).start()
 
     def rows(start, count):
         return pl.ds(pl.multiple_of(start, 8), count)
 
+    def tally(ssem, rsem, count):
+        ref = full.at[pl.ds(0, count)]
+        return pltpu.make_async_remote_copy(src_ref=ref, dst_ref=ref, send_sem=ssem, recv_sem=rsem,
+                                            device_id=at_c(), device_id_type=MESH)
+
+    def arrived(rsem, count):
+        tally(send_sem.at[0], rsem, count).wait_recv()
+
     chunk = piece * nx
 
     def chunk_of(core, yy):
@@ -245,63 +285,77 @@
 
     far = [o for o in RING8 if o < ny] + [0]
     targets = [lax.rem(y + o, ny) for o in far]
-    copies_c = [send(part.at[chunk_of(1 - c, t)], buf_c.at[i], send_c.at[i], recv_c.at[i], at_c())
-                for i, t in enumerate(targets)]
-    copies_x = []
-    for i, t in enumerate(targets):
-        copies_c[i].wait_recv()
-        acc_c[i] = part[chunk_of(c, t), :] + buf_c[i]
-        copies_x.append([
-            send(acc_c.at[i, rows(lax.rem(x + o, nx) * piece, piece)], buf_x.at[i, o - 1],
-                 send_x.at[i, o - 1], recv_x.at[i, o - 1], at_x(o)) for o in (2, 1, 3) if o < nx])
-    copies_y = []
-    for i, o in enumerate(far):
-        for copy in copies_x[i]:
-            copy.wait_recv()
-        total = acc_c[i, rows(x * piece, piece), :]
-        for k in range(nx - 1):
-            total = total + buf_x[i, k]
-        acc_x[i] = total
-        if o:
-            copies_y.append(send(acc_x.at[i], buf_y.at[o - 1], send_y.at[o - 1], recv_y.at[o - 1], at_y(o)))
-    for copy in copies_y:
-        copy.wait_recv()
+    for g, members in enumerate(OUTWARD):
+        for i in members:
+            send(part.at[chunk_of(1 - c, targets[i])], buf_c.at[i], send_sem.at[0], recv_c.at[g], at_c())
+    for g, members in enumerate(OUTWARD):
+        arrived(recv_c.at[g], len(members) * chunk)
+        for i in members:
+            acc_c[i] = part[chunk_of(c, targets[i]), :] + buf_c[i]
+        for o in (2, 1, 3):
+            for i in members:
+                send(acc_c.at[i, rows(lax.rem(x + o, nx) * piece, piece)], buf_x.at[i, o - 1],
+                     send_sem.at[1], recv_x.at[g], at_x(o))
+    for g, members in enumerate(OUTWARD):
+        arrived(recv_x.at[g], len(members) * piece * (nx - 1))
+        for i in members:
+            total = acc_c[i, rows(x * piece, piece), :]
+            for k in range(nx - 1):
+                total = total + buf_x[i, k]
+            acc_x[i] = total
+        for i in members:
+            if far[i]:
+                send(acc_x.at[i], buf_y.at[far[i] - 1], send_sem.at[2], recv_y.at[0], at_y(far[i]))
+    arrived(recv_y.at[0], piece * (ny - 1))
+    total = acc_x[ny - 1]
     for k in range(ny - 1):
         total = total + buf_y[k]
     acc_y[...] = total
-    copies_z = [send(acc_y, buf_z.at[z], send_z.at[o - 1], recv_z.at[o - 1], at_z(o)) for o in RING8 if o < nz]
+    for o in RING8:
+        send(acc_y, buf_z.at[z], send_sem.at[3], recv_z.at[0], at_z(o))
     buf_z[z] = total
-    for copy in copies_z:
-        copy.wait_recv()
+    arrived(recv_z.at[0], piece * (nz - 1))
     total = buf_z[0]
     for k in range(1, nz):
         total = total + buf_z[k]
     mine = full.at[piece_of(c, y, x)]
     mine[...] = total
-    gather_y = {o: send(mine, mine, gsend_y.at[o - 1], grecv_y.at[o - 1], at_y(o)) for o in RING8 if o < ny}
-    near = [0] + [o for o in RING8[::-1] if o < ny]
-    sources = [lax.rem(y - o + ny, ny) for o in near]
-    gather_x = []
-    for i, o in enumerate(near):
-        if o:
-            gather_y[o].wait_recv()
-        ref = full.at[piece_of(c, sources[i], x)]
-        gather_x.append([send(ref, ref, gsend_x.at[i, k - 1], grecv_x.at[i, k - 1], at_x(k))
-                         for k in (2, 1, 3) if k < nx])
-    gather_c = []
-    for i in range(ny):
-        for copy in gather_x[i]:
-            copy.wait_recv()
-        ref = full.at[chunk_of(c, sources[i])]
-        gather_c.append(send(ref, ref, gsend_c.at[i], grecv_c.at[i], at_c()))
-    for copy in gather_c:
-        copy.wait_recv()
-    assemble(full, mat, scale, root, ridge)
-    eliminate(mat)
+    for o in RING8:
+        send(mine, mine, send_sem.at[4], grecv_y.at[0], at_y(o))
+    arrived(grecv_y.at[0], piece * (ny - 1))
+    for g, members in enumerate(HOMEWARD):
+        for o in (2, 1, 3):
+            for yy in members:
+                ref = full.at[piece_of(c, yy, x)]
+                send(ref, ref, send_sem.at[5], grecv_x.at[g], at_x(o))
+
+    def to_core(g):
+        members = HOMEWARD[g]
+        arrived(grecv_x.at[g], len(members) * piece * (nx - 1))
+        ref = full.at[rows((c * ny + members[0]) * chunk, len(members) * chunk)]
+        send(ref, ref, send_sem.at[6], grecv_c.at[g], at_c())
+
+    def landed(g):
+        arrived(grecv_c.at[g], len(HOMEWARD[g]) * chunk)
+
+    to_core(0)
+    landed(0)
+    assemble(full, mat, scale, root, ridge, 0, 1)
+
+    def between(step):
+        if step == MIDWAY:
+            to_core(1)
+
+    def rest():
+        landed(1)
+        assemble(full, mat, scale, root, ridge, 1, 10)
+
+    eliminate(mat, between, rest)
     block = mat[pl.ds(pl.multiple_of(x * 128, 128), 128), 512:640]
     out_ref[...] = block.T[0:1, :]
-    for copy in sends:
-        copy.wait_send()
+    for n, count in enumerate((chunk * ny, piece * ny * (nx - 1), piece * (ny - 1), piece * (nz - 1), piece * (ny - 1),
+                               piece * ny * (nx - 1), chunk * ny)):
+        tally(send_sem.at[n], recv_c.at[0], count).wait_send()
 
 
 def fit(consts, nx, ny, nz, p, cyc, az, b, src):
@@ -311,9 +365,6 @@
     anywhere = pl.BlockSpec(memory_space=pl.ANY)
     dma = pltpu.SemaphoreType.DMA
     v = pltpu.VMEM
-
-    def pair(*shape):
-        return [dma(shape), dma(shape)]
 
     return pl.pallas_call(
         functools.partial(fit_kernel, (nx, ny, nz, piece), consts),
@@ -328,8 +379,7 @@
             v((ny, piece * nx, 128), F32), v((ny, piece, 128), F32), v((piece, 128), F32),
             v((ny, piece * nx, 128), F32), v((ny, nx - 1, piece, 128), F32), v((ny - 1, piece, 128), F32),
             v((nz, piece, 128), F32),
-            *pair(ny), *pair(ny, nx - 1), *pair(ny - 1), *pair(nz - 1),
-            *pair(ny), *pair(ny, nx - 1), *pair(ny - 1),
+            dma((7,)), *[dma((ny,))] * 7,
         ],
         name="fit",
         compiler_params=pltpu.CompilerParams(collective_id=0, has_side_effects=True, vmem_limit_bytes=56 << 20),

time: 59.5 us -> 58.9 us (0.990)
  Pallas kernels: 57.5 us -> 56.9 us
where the time goes in v4:
time: 58.9 us; the launch traced here: 58.8 us
  Pallas kernels  56.9 us (97%)
  local copies, waits for them, and re-layouts  1.19 us (2%)
  between operations  0.66 us (1%)
    pallas_call x1, Pallas kernels, fit(): pl.pallas_call(functools.partial(fit_kernel, (nx, ny, nz, piece), consts)...  56.9 us
    unnamed x1, local copies, waits for them, and re-layouts  1.19 us

profile of v4, /device:TPU:1, one launch (start us, length us, event | category | flops | bytes accessed | tf_op | source)
XLA Modules:
  0.0 58.8 jit_solution(4621276773375650393)
XLA Ops:
  0.7 56.9 %fit.1 = f32[1,128]{1,0:T(1,128)} custom-call(s32[1]{0:T(128)S(6)} %copy.7.bin_hbm, f32[1,2048]{1,0:T(1,128)} %p_hbm.1, s32[1,2048]{1,0:T(1,128)} %cyc_hbm.1, s32[1,2048]{1,0:T(1,128)} %az_hbm.1, s32[1,512]{1,0:T(1,128)} %bitcast.1), custom_call_target="tpu_custom_call" | custom-call | tf_op jit(solution)/shard_map/fit/pallas_call | solution.py:369
  57.6 1.2 %copy.8 = f32[1,128]{1,0:T(1,128)} copy(f32[1,128]{1,0:T(1,128)} %fit.1) | data formatting | bytes 1024

commit v5 on v4

--- a/solution.py
+++ b/solution.py
@@ -13,7 +13,7 @@
 S = 512
 NRING = 4096
 NAZ = 8192
-PAIRS = [(i, j) for i in range(4) for j in range(i, 4)]
+CROSS = [(i, j) for i in range(4) for j in range(i + 1, 4)]
 
 NT=(((1,),(1,)),((),()))
 CHUNK=512
@@ -109,13 +109,20 @@
     def lblk(i,j):
         m=L1 if j<2 else L2
         return m[at(i):at(i)+128,128*(j%2):128*(j%2)+128]
-    for k,(i,j) in enumerate(PAIRS):
-        out_ref[128*k:128*k+128,:]=((hblk(i,j)+lblk(i,j))+lblk(j,i).T)*gain
+    def gram(i,j):
+        return ((hblk(i,j)+lblk(i,j))+lblk(j,i).T)*gain
+    ri=lax.broadcasted_iota(jnp.int32,(128,128),0); ci=lax.broadcasted_iota(jnp.int32,(128,128),1)
+    diagonals=[]
+    for n,i in ((0,0),(7,2)):
+        other=gram(i+1,i+1)
+        out_ref[128*n:128*n+128,:]=jnp.where(ri<=ci,gram(i,i),other)
+        diagonals.append(jnp.sum(jnp.where(ri==ci,other,0.0),axis=0,keepdims=True))
+    for n,(i,j) in enumerate(CROSS):
+        out_ref[128*(n+1):128*(n+1)+128,:]=gram(i,j)
     r1=(H1[HALF:HALF+1]+L1[HALF:HALF+1])+(H1[HALF+1:HALF+2]+L1[HALF+1:HALF+2])
     r2=(H2[HALF:HALF+1]+L2[HALF:HALF+1])+(H2[HALF+1:HALF+2]+L2[HALF+1:HALF+2])
-    tail=jnp.concatenate([r1[:,:128],r1[:,128:],r2[:,:128],r2[:,128:],jnp.zeros((4,128),F32)],axis=0)
-    out_ref[1280:1288,:]=tail*unit
-    out_ref[1288:1536,:]=jnp.zeros((248,128),F32)
+    tail=jnp.concatenate([r1[:,:128],r1[:,128:],r2[:,:128],r2[:,128:]],axis=0)*unit
+    out_ref[1024:1032,:]=jnp.concatenate([tail]+diagonals+[jnp.zeros((2,128),F32)],axis=0)
 
 TERMS=6; INNER=3; SG=16
 def dot(a,b): return jnp.dot(a,b,preferred_element_type=F32)
@@ -201,30 +208,37 @@
             mat[128*o:128*o+128,b+128:]-=mm(mat[128*o:128*o+128,b:b+128],R)
         mat[b:b+128,b+128:]=R
 
-def assemble(red_ref, mat, scale, root, ridge, start, stop):
+def assemble(red_ref, last, mat, scale, root, ridge, first):
     r=lax.broadcasted_iota(jnp.int32,(128,128),0); c=lax.broadcasted_iota(jnp.int32,(128,128),1)
-    for n in range(start,stop):
-        i,j=PAIRS[n]
-        b=red_ref[128*n:128*n+128,:]*scale
-        if i==j: b=b+jnp.where(r==c,ridge,0.0)
+    def pair_of(n, diagonal):
+        b=red_ref[128*n:128*n+128,:]
+        t=b.T
+        one=jnp.where(r<=c,b,t); two=jnp.where(r>c,b,jnp.where(r==c,last[diagonal:diagonal+1,:],t))
+        return [v*scale+jnp.where(r==c,ridge,0.0) for v in (one,two)]
+    if first:
+        mat[0:128,0:128]=pair_of(0,4)[0]
+        return
+    mat[128:256,128:256]=pair_of(0,4)[1]
+    mat[256:384,256:384],mat[384:512,384:512]=pair_of(7,5)
+    for n,(i,j) in enumerate(CROSS):
+        b=red_ref[128*(n+1):128*(n+1)+128,:]*scale
         mat[128*i:128*i+128,128*j:128*j+128]=b
-        if i!=j: mat[128*j:128*j+128,128*i:128*i+128]=b.T
-    if stop==len(PAIRS):
-        for i in range(4):
-            row=red_ref[1280+i:1281+i,:]*root
-            mat[128*i:128*i+128,512:640]=jnp.broadcast_to(row,(128,128)).T
+        mat[128*j:128*j+128,128*i:128*i+128]=b.T
+    for i in range(4):
+        row=last[i:i+1,:]*root
+        mat[128*i:128*i+128,512:640]=jnp.broadcast_to(row,(128,128)).T
 
 MESH = pl.DeviceIdType.MESH
 RING8 = (4, 3, 5, 2, 6, 1, 7)
 OUTWARD = tuple((i,) for i in range(8))
 HOMEWARD = ((0, 1), (2, 3, 4, 5, 6, 7))
-MIDWAY = 3
+MIDWAY = 5
 
 
 def fit_kernel(dims, consts, bin_hbm, p_hbm, cyc_hbm, az_hbm, src_hbm, out_ref,
                bin_ref, p_ref, cyc_ref, az_ref, src_ref, in_sem, src_scr, mic_scr, hi_scr, lo_scr,
-               part, full, mat, acc_c, acc_x, acc_y, buf_c, buf_x, buf_y, buf_z,
-               send_sem, recv_c, recv_x, recv_y, recv_z, grecv_y, grecv_x, grecv_c):
+               part, full, mat, last, acc_c, acc_e, acc_x, acc_y, buf_c, buf_ec, buf_x, buf_ex, buf_y, buf_z,
+               send_sem, recv_e, recv_c, recv_x, recv_y, recv_z, grecv_y, grecv_x, grecv_c):
     nx, ny, nz, piece = dims
     x = lax.axis_index("grp")
     row = lax.axis_index("row")
@@ -285,9 +299,17 @@
 
     far = [o for o in RING8 if o < ny] + [0]
     targets = [lax.rem(y + o, ny) for o in far]
+    body = chunk * ny * 2
+    extra = part.at[pl.ds(body, 8)]
+    send(extra, buf_ec, send_sem.at[0], recv_e.at[0], at_c())
     for g, members in enumerate(OUTWARD):
         for i in members:
             send(part.at[chunk_of(1 - c, targets[i])], buf_c.at[i], send_sem.at[0], recv_c.at[g], at_c())
+    arrived(recv_e.at[0], 8)
+    acc_e[...] = extra[...] + buf_ec[...]
+    buf_ex[x] = acc_e[...]
+    for o in (2, 1, 3):
+        send(acc_e, buf_ex.at[x], send_sem.at[1], recv_e.at[1], at_x(o))
     for g, members in enumerate(OUTWARD):
         arrived(recv_c.at[g], len(members) * chunk)
         for i in members:
@@ -296,30 +318,39 @@
             for i in members:
                 send(acc_c.at[i, rows(lax.rem(x + o, nx) * piece, piece)], buf_x.at[i, o - 1],
                      send_sem.at[1], recv_x.at[g], at_x(o))
+    arrived(recv_e.at[1], 8 * (nx - 1))
+    spread = buf_ex[0]
+    for k in range(1, nx):
+        spread = spread + buf_ex[k]
     for g, members in enumerate(OUTWARD):
         arrived(recv_x.at[g], len(members) * piece * (nx - 1))
         for i in members:
             total = acc_c[i, rows(x * piece, piece), :]
             for k in range(nx - 1):
                 total = total + buf_x[i, k]
-            acc_x[i] = total
-        for i in members:
             if far[i]:
-                send(acc_x.at[i], buf_y.at[far[i] - 1], send_sem.at[2], recv_y.at[0], at_y(far[i]))
-    arrived(recv_y.at[0], piece * (ny - 1))
-    total = acc_x[ny - 1]
-    for k in range(ny - 1):
+                acc_x[i, 0:piece, :] = total
+                acc_x[i, piece:piece + 8, :] = spread
+                send(acc_x.at[i], buf_y.at[y], send_sem.at[2], recv_y.at[0], at_y(far[i]))
+            else:
+                buf_y[y, 0:piece, :] = total
+                buf_y[y, piece:piece + 8, :] = spread
+    wide = piece + 8
+    arrived(recv_y.at[0], wide * (ny - 1))
+    total = buf_y[0]
+    for k in range(1, ny):
         total = total + buf_y[k]
     acc_y[...] = total
     for o in RING8:
         send(acc_y, buf_z.at[z], send_sem.at[3], recv_z.at[0], at_z(o))
     buf_z[z] = total
-    arrived(recv_z.at[0], piece * (nz - 1))
+    arrived(recv_z.at[0], wide * (nz - 1))
     total = buf_z[0]
     for k in range(1, nz):
         total = total + buf_z[k]
     mine = full.at[piece_of(c, y, x)]
-    mine[...] = total
+    mine[...] = total[0:piece]
+    last[...] = total[piece:wide]
     for o in RING8:
         send(mine, mine, send_sem.at[4], grecv_y.at[0], at_y(o))
     arrived(grecv_y.at[0], piece * (ny - 1))
@@ -340,7 +371,7 @@
 
     to_core(0)
     landed(0)
-    assemble(full, mat, scale, root, ridge, 0, 1)
+    assemble(full, last, mat, scale, root, ridge, True)
 
     def between(step):
         if step == MIDWAY:
@@ -348,19 +379,19 @@
 
     def rest():
         landed(1)
-        assemble(full, mat, scale, root, ridge, 1, 10)
+        assemble(full, last, mat, scale, root, ridge, False)
 
     eliminate(mat, between, rest)
     block = mat[pl.ds(pl.multiple_of(x * 128, 128), 128), 512:640]
     out_ref[...] = block.T[0:1, :]
-    for n, count in enumerate((chunk * ny, piece * ny * (nx - 1), piece * (ny - 1), piece * (nz - 1), piece * (ny - 1),
+    for n, count in enumerate((chunk * ny + 8, (piece * ny + 8) * (nx - 1), wide * (ny - 1), wide * (nz - 1), piece * (ny - 1),
                                piece * ny * (nx - 1), chunk * ny)):
         tally(send_sem.at[n], recv_c.at[0], count).wait_send()
 
 
 def fit(consts, nx, ny, nz, p, cyc, az, b, src):
     n = p.shape[1]
-    rows = 1536
+    rows = 1024
     piece = rows // (2 * nx * ny)
     anywhere = pl.BlockSpec(memory_space=pl.ANY)
     dma = pltpu.SemaphoreType.DMA
@@ -375,11 +406,11 @@
             pltpu.SMEM((1,), jnp.int32), v((1, n), F32), v((1, n), jnp.int32), v((1, n), jnp.int32),
             v((1, S), jnp.int32), dma((5,)),
             v((S, 128), BF), v((16, n), BF), v((S + 16, n), BF), v((S, n), BF),
-            v((rows, 128), F32), v((rows, 128), F32), v((512, 640), F32),
-            v((ny, piece * nx, 128), F32), v((ny, piece, 128), F32), v((piece, 128), F32),
-            v((ny, piece * nx, 128), F32), v((ny, nx - 1, piece, 128), F32), v((ny - 1, piece, 128), F32),
-            v((nz, piece, 128), F32),
-            dma((7,)), *[dma((ny,))] * 7,
+            v((rows + 8, 128), F32), v((rows, 128), F32), v((512, 640), F32), v((8, 128), F32),
+            v((ny, piece * nx, 128), F32), v((8, 128), F32), v((ny, piece + 8, 128), F32), v((piece + 8, 128), F32),
+            v((ny, piece * nx, 128), F32), v((8, 128), F32), v((ny, nx - 1, piece, 128), F32), v((nx, 8, 128), F32),
+            v((ny, piece + 8, 128), F32), v((nz, piece + 8, 128), F32),
+            dma((7,)), dma((2,)), *[dma((ny,))] * 7,
         ],
         name="fit",
         compiler_params=pltpu.CompilerParams(collective_id=0, has_side_effects=True, vmem_limit_bytes=56 << 20),

time: 58.9 us -> 57 us (0.968)
  Pallas kernels: 56.9 us -> 55 us
    pallas_call x1, Pallas kernels: 56.9 us -> 55 us  [fit(): pl.pallas_call(functools.partial(fit_kernel, (nx, ny, nz, piece), consts)...]
where the time goes in v5:
time: 57 us; the launch traced here: 56.8 us
  Pallas kernels  55 us (96%)
  local copies, waits for them, and re-layouts  1.19 us (2%)
  between operations  0.66 us (1%)
    pallas_call x1, Pallas kernels, fit(): pl.pallas_call(functools.partial(fit_kernel, (nx, ny, nz, piece), consts)...  55 us
    unnamed x1, local copies, waits for them, and re-layouts  1.19 us

profile of v5, /device:TPU:1, one launch (start us, length us, event | category | flops | bytes accessed | tf_op | source)
XLA Modules:
  0.0 56.8 jit_solution(1508098492480229646)
XLA Ops:
  0.7 55.0 %fit.1 = f32[1,128]{1,0:T(1,128)} custom-call(s32[1]{0:T(128)S(6)} %copy.7.bin_hbm, f32[1,2048]{1,0:T(1,128)} %p_hbm.1, s32[1,2048]{1,0:T(1,128)} %cyc_hbm.1, s32[1,2048]{1,0:T(1,128)} %az_hbm.1, s32[1,512]{1,0:T(1,128)} %bitcast.1), custom_call_target="tpu_custom_call" | custom-call | tf_op jit(solution)/shard_map/fit/pallas_call | solution.py:400
  55.7 1.2 %copy.8 = f32[1,128]{1,0:T(1,128)} copy(f32[1,128]{1,0:T(1,128)} %fit.1) | data formatting | bytes 1024

commit v6 on v5

--- a/solution.py
+++ b/solution.py
@@ -232,7 +232,7 @@
 RING8 = (4, 3, 5, 2, 6, 1, 7)
 OUTWARD = tuple((i,) for i in range(8))
 HOMEWARD = ((0, 1), (2, 3, 4, 5, 6, 7))
-MIDWAY = 5
+MIDWAY = 6
 
 
 def fit_kernel(dims, consts, bin_hbm, p_hbm, cyc_hbm, az_hbm, src_hbm, out_ref,
@@ -258,7 +258,7 @@
     def at_z(o):
         return {"row": row + 2 * ny * (lax.rem(z + o, nz) - z)}
 
-    partners = [at_c()] + [at_x(o) for o in range(1, nx)] + [at_y(o) for o in range(1, ny)]
+    partners = [{"grp": lax.rem(x + o, nx), "row": row + 1 - 2 * c} for o in range(nx)] + [at_x(o) for o in range(1, nx)] + [at_y(o) for o in range(1, ny)]
     partners += [at_z(o) for o in range(1, nz)]
     barrier = pltpu.get_barrier_semaphore()
     for partner in partners:
@@ -352,13 +352,22 @@
     mine[...] = total[0:piece]
     last[...] = total[piece:wide]
     for o in RING8:
-        send(mine, mine, send_sem.at[4], grecv_y.at[0], at_y(o))
-    arrived(grecv_y.at[0], piece * (ny - 1))
-    for g, members in enumerate(HOMEWARD):
-        for o in (2, 1, 3):
-            for yy in members:
-                ref = full.at[piece_of(c, yy, x)]
-                send(ref, ref, send_sem.at[5], grecv_x.at[g], at_x(o))
+        send(mine, mine, send_sem.at[4], grecv_y.at[o - 1], at_y(o))
+    early = len(HOMEWARD[0])
+    for o in (0,) + RING8[::-1]:
+        if o:
+            arrived(grecv_y.at[o - 1], piece)
+        source = lax.rem(y - o + ny, ny)
+        ref = full.at[piece_of(c, source, x)]
+        group = (source + ny - early) // ny
+        for k in (2, 1, 3):
+            send(ref, ref, send_sem.at[5], grecv_x.at[group], at_x(k))
+
+        @pl.when(source < early)
+        def _():
+            for k in (2, 1, 3, 0):
+                across = {"grp": lax.rem(x + k, nx), "row": row + 1 - 2 * c}
+                send(ref, ref, send_sem.at[5], grecv_x.at[0], across)
 
     def to_core(g):
         members = HOMEWARD[g]
@@ -369,8 +378,7 @@
     def landed(g):
         arrived(grecv_c.at[g], len(HOMEWARD[g]) * chunk)
 
-    to_core(0)
-    landed(0)
+    arrived(grecv_x.at[0], early * piece * (2 * nx - 1))
     assemble(full, last, mat, scale, root, ridge, True)
 
     def between(step):
@@ -385,7 +393,7 @@
     block = mat[pl.ds(pl.multiple_of(x * 128, 128), 128), 512:640]
     out_ref[...] = block.T[0:1, :]
     for n, count in enumerate((chunk * ny + 8, (piece * ny + 8) * (nx - 1), wide * (ny - 1), wide * (nz - 1), piece * (ny - 1),
-                               piece * ny * (nx - 1), chunk * ny)):
+                               piece * (ny * (nx - 1) + early * nx), chunk * (ny - early))):
         tally(send_sem.at[n], recv_c.at[0], count).wait_send()
 
 

time: 57 us -> 55.9 us (0.981)
  Pallas kernels: 55 us -> 53.9 us
    pallas_call x1, Pallas kernels: 55 us -> 53.9 us  [fit(): pl.pallas_call(functools.partial(fit_kernel, (nx, ny, nz, piece), consts)...]
where the time goes in v6:
time: 55.9 us; the launch traced here: 55.7 us
  Pallas kernels  53.9 us (96%)
  local copies, waits for them, and re-layouts  1.19 us (2%)
  between operations  0.66 us (1%)
    pallas_call x1, Pallas kernels, fit(): pl.pallas_call(functools.partial(fit_kernel, (nx, ny, nz, piece), consts)...  53.9 us
    unnamed x1, local copies, waits for them, and re-layouts  1.19 us

profile of v6, /device:TPU:1, one launch (start us, length us, event | category | flops | bytes accessed | tf_op | source)
XLA Modules:
  0.0 55.7 jit_solution(5287640708091641781)
XLA Ops:
  0.7 53.9 %fit.1 = f32[1,128]{1,0:T(1,128)} custom-call(s32[1]{0:T(128)S(6)} %copy.7.bin_hbm, f32[1,2048]{1,0:T(1,128)} %p_hbm.1, s32[1,2048]{1,0:T(1,128)} %cyc_hbm.1, s32[1,2048]{1,0:T(1,128)} %az_hbm.1, s32[1,512]{1,0:T(1,128)} %bitcast.1), custom_call_target="tpu_custom_call" | custom-call | tf_op jit(solution)/shard_map/fit/pallas_call | solution.py:408
  54.5 1.2 %copy.8 = f32[1,128]{1,0:T(1,128)} copy(f32[1,128]{1,0:T(1,128)} %fit.1) | data formatting | bytes 1024

commit v7 on v6

--- a/solution.py
+++ b/solution.py
@@ -16,7 +16,7 @@
 CROSS = [(i, j) for i in range(4) for j in range(i + 1, 4)]
 
 NT=(((1,),(1,)),((),()))
-CHUNK=512
+CHUNK=256
 SINE=(6.283185160089467, -41.341655031414675, 81.60100407316348, -76.54978229140988, 39.5367060495799)
 MAGIC=12582912.0
 
@@ -85,22 +85,29 @@
     loads[4].wait()
     ph,pm=[v.astype(F32) for v in split(p_ref[...],2)]
     hi_scr[HALF:HALF+16,:]=jnp.concatenate([ph,pm]+[jnp.zeros_like(ph)]*14,axis=0).astype(BF)
-    for lo in range(0, S, HALF):
-        for c in range(n//CHUNK):
-            cols=slice(c*CHUNK,(c+1)*CHUNK)
-            t2=jnp.dot(src_scr[lo:lo+HALF,:16],mic_scr[:,cols],preferred_element_type=F32)
-            r=lax.rsqrt(t2)
-            val=cos_turns(t2*r, r)
-            h=val.astype(BF)
-            hi_scr[lo+(16 if lo else 0):lo+(16 if lo else 0)+HALF,cols]=h
-            lo_scr[lo:lo+HALF,cols]=(val-h.astype(F32)).astype(BF)
-    unit=1.5*(bin_ref[0].astype(F32)+1.0)*float(1/(2*np.pi))
-    gain=unit*unit
+    def fill(lo, c):
+        cols=slice(c*CHUNK,(c+1)*CHUNK)
+        t2=jnp.dot(src_scr[lo:lo+HALF,:16],mic_scr[:,cols],preferred_element_type=F32)
+        r=lax.rsqrt(t2)
+        val=cos_turns(t2*r, r)
+        h=val.astype(BF)
+        base=lo+(16 if lo else 0)
+        hi_scr[base:base+HALF,cols]=h
+        lo_scr[lo:lo+HALF,cols]=(val-h.astype(F32)).astype(BF)
     def product(a, b):
         return lax.dot_general(a, b, NT, preferred_element_type=F32)
     R0=HALF+16
-    H1=product(hi_scr[0:R0],hi_scr[0:HALF]); L1=product(hi_scr[...],lo_scr[0:HALF])
-    H2=product(hi_scr[...],hi_scr[R0:]); L2=product(hi_scr[...],lo_scr[HALF:S])
+    unit=1.5*(bin_ref[0].astype(F32)+1.0)*float(1/(2*np.pi))
+    gain=unit*unit
+    H1=L1=H2=L2=None
+    for c in range(n//CHUNK+1):
+        if c<n//CHUNK:
+            fill(0, c); fill(HALF, c)
+        if c:
+            k=slice((c-1)*CHUNK,c*CHUNK)
+            new=[product(hi_scr[0:R0,k],hi_scr[0:HALF,k]),product(hi_scr[:,k],lo_scr[0:HALF,k]),product(hi_scr[:,k],hi_scr[R0:,k]),product(hi_scr[:,k],lo_scr[HALF:S,k])]
+            if H1 is not None: new=[u+v for u,v in zip((H1,L1,H2,L2),new)]
+            H1,L1,H2,L2=new
     def at(i):
         return 128*i+(16 if i>=2 else 0)
     def hblk(i,j):
@@ -191,21 +198,22 @@
         M=put(R,p0,M)
     return M
 
-def eliminate(mat, between, rest):
+def eliminate(mat, between, rest, me):
     for k in range(4):
         b=128*k
         Mi=invert(mat[b:b+128,b:b+128], between if k==0 else None)
         if k==0:
             rest()
         R=mm(Mi,mat[b:b+128,b+128:])
-        order=[(k+1+t)%4 for t in range(3)]
-        if k<3:
-            o=k+1
-            mat[128*o:128*o+128,128*o:128*o+128]-=mm(mat[128*o:128*o+128,b:b+128],R[:,:128])
-            mat[128*o:128*o+128,128*o+128:]-=mm(mat[128*o:128*o+128,b:b+128],R[:,128:])
-            order=order[1:]
-        for o in order:
-            mat[128*o:128*o+128,b+128:]-=mm(mat[128*o:128*o+128,b:b+128],R)
+        if k==3:
+            mine=pl.ds(pl.multiple_of(me*128,128),128)
+            return jnp.where(me==3,R,mat[mine,512:640]-mm(mat[mine,b:b+128],R))
+        o=k+1
+        mat[128*o:128*o+128,128*o:128*o+128]-=mm(mat[128*o:128*o+128,b:b+128],R[:,:128])
+        mat[128*o:128*o+128,128*o+128:]-=mm(mat[128*o:128*o+128,b:b+128],R[:,128:])
+        for o in range(4):
+            if o not in (k,k+1):
+                mat[128*o:128*o+128,b+128:]-=mm(mat[128*o:128*o+128,b:b+128],R)
         mat[b:b+128,b+128:]=R
 
 def assemble(red_ref, last, mat, scale, root, ridge, first):
@@ -233,6 +241,7 @@
 OUTWARD = tuple((i,) for i in range(8))
 HOMEWARD = ((0, 1), (2, 3, 4, 5, 6, 7))
 MIDWAY = 6
+LAND = 8
 
 
 def fit_kernel(dims, consts, bin_hbm, p_hbm, cyc_hbm, az_hbm, src_hbm, out_ref,
@@ -381,16 +390,17 @@
     arrived(grecv_x.at[0], early * piece * (2 * nx - 1))
     assemble(full, last, mat, scale, root, ridge, True)
 
+    def rest():
+        landed(1)
+        assemble(full, last, mat, scale, root, ridge, False)
+
     def between(step):
         if step == MIDWAY:
             to_core(1)
-
-    def rest():
-        landed(1)
-        assemble(full, last, mat, scale, root, ridge, False)
-
-    eliminate(mat, between, rest)
-    block = mat[pl.ds(pl.multiple_of(x * 128, 128), 128), 512:640]
+        if step == LAND:
+            rest()
+
+    block = eliminate(mat, between, rest if LAND == 8 else lambda: None, x)
     out_ref[...] = block.T[0:1, :]
     for n, count in enumerate((chunk * ny + 8, (piece * ny + 8) * (nx - 1), wide * (ny - 1), wide * (nz - 1), piece * (ny - 1),
                                piece * (ny * (nx - 1) + early * nx), chunk * (ny - early))):

time: 55.9 us -> 55.1 us (0.986)
  Pallas kernels: 53.9 us -> 53 us
    pallas_call x1, Pallas kernels: 53.9 us -> 53 us  [fit(): pl.pallas_call(functools.partial(fit_kernel, (nx, ny, nz, piece), consts)...]
where the time goes in v7:
time: 55.1 us; the launch traced here: 54.9 us
  Pallas kernels  53 us (96%)
  local copies, waits for them, and re-layouts  1.19 us (2%)
  between operations  0.66 us (1%)
    pallas_call x1, Pallas kernels, fit(): pl.pallas_call(functools.partial(fit_kernel, (nx, ny, nz, piece), consts)...  53 us
    unnamed x1, local copies, waits for them, and re-layouts  1.19 us

profile of v7, /device:TPU:1, one launch (start us, length us, event | category | flops | bytes accessed | tf_op | source)
XLA Modules:
  0.0 54.9 jit_solution(4381965106079896307)
XLA Ops:
  0.7 53.0 %fit.1 = f32[1,128]{1,0:T(1,128)} custom-call(s32[1]{0:T(128)S(6)} %copy.7.bin_hbm, f32[1,2048]{1,0:T(1,128)} %p_hbm.1, s32[1,2048]{1,0:T(1,128)} %cyc_hbm.1, s32[1,2048]{1,0:T(1,128)} %az_hbm.1, s32[1,512]{1,0:T(1,128)} %bitcast.1), custom_call_target="tpu_custom_call" | custom-call | tf_op jit(solution)/shard_map/fit/pallas_call | solution.py:418
  53.7 1.2 %copy.8 = f32[1,128]{1,0:T(1,128)} copy(f32[1,128]{1,0:T(1,128)} %fit.1) | data formatting | bytes 1024

commit v8 on v7

--- a/solution.py
+++ b/solution.py
@@ -267,18 +267,18 @@
     def at_z(o):
         return {"row": row + 2 * ny * (lax.rem(z + o, nz) - z)}
 
-    partners = [{"grp": lax.rem(x + o, nx), "row": row + 1 - 2 * c} for o in range(nx)] + [at_x(o) for o in range(1, nx)] + [at_y(o) for o in range(1, ny)]
-    partners += [at_z(o) for o in range(1, nz)]
-    barrier = pltpu.get_barrier_semaphore()
-    for partner in partners:
-        pl.semaphore_signal(barrier, inc=1, device_id=partner, device_id_type=MESH)
-
     loads = []
     for n, (src, dst) in enumerate([(src_hbm, src_ref), (cyc_hbm, cyc_ref), (az_hbm, az_ref), (bin_hbm, bin_ref),
                                     (p_hbm, p_ref)]):
         load = pltpu.make_async_copy(src, dst, in_sem.at[n])
         load.start()
         loads.append(load)
+    partners = [{"grp": lax.rem(x + o, nx), "row": row + 1 - 2 * c} for o in range(nx)] + [at_x(o) for o in range(1, nx)] + [at_y(o) for o in range(1, ny)]
+    partners += [at_z(o) for o in range(1, nz)]
+    barrier = pltpu.get_barrier_semaphore()
+    for partner in partners:
+        pl.semaphore_signal(barrier, inc=1, device_id=partner, device_id_type=MESH)
+
     scale, root, ridge, spacing = consts
     panel_gram(loads, spacing, bin_ref, p_ref, cyc_ref, az_ref, src_ref, part, src_scr, mic_scr, hi_scr, lo_scr)
     pl.semaphore_wait(barrier, len(partners))

time: 55.1 us -> 54.8 us (level)
  no operation moved by 1% of the time
where the time goes in v8:
time: 54.8 us; the launch traced here: 54.7 us
  Pallas kernels  52.8 us (96%)
  local copies, waits for them, and re-layouts  1.19 us (2%)
  between operations  0.66 us (1%)
    pallas_call x1, Pallas kernels, fit(): pl.pallas_call(functools.partial(fit_kernel, (nx, ny, nz, piece), consts)...  52.8 us
    unnamed x1, local copies, waits for them, and re-layouts  1.19 us

profile of v8, /device:TPU:1, one launch (start us, length us, event | category | flops | bytes accessed | tf_op | source)
XLA Modules:
  0.0 54.7 jit_solution(10254443764200136993)
XLA Ops:
  0.7 52.8 %fit.1 = f32[1,128]{1,0:T(1,128)} custom-call(s32[1]{0:T(128)S(6)} %copy.7.bin_hbm, f32[1,2048]{1,0:T(1,128)} %p_hbm.1, s32[1,2048]{1,0:T(1,128)} %cyc_hbm.1, s32[1,2048]{1,0:T(1,128)} %az_hbm.1, s32[1,512]{1,0:T(1,128)} %bitcast.1), custom_call_target="tpu_custom_call" | custom-call | tf_op jit(solution)/shard_map/fit/pallas_call | solution.py:418
  53.5 1.2 %copy.8 = f32[1,128]{1,0:T(1,128)} copy(f32[1,128]{1,0:T(1,128)} %fit.1) | data formatting | bytes 1024

commit v9 on v8

--- a/solution.py
+++ b/solution.py
@@ -204,13 +204,15 @@
         Mi=invert(mat[b:b+128,b:b+128], between if k==0 else None)
         if k==0:
             rest()
-        R=mm(Mi,mat[b:b+128,b+128:])
+        near=mm(Mi,mat[b:b+128,b+128:b+256])
         if k==3:
             mine=pl.ds(pl.multiple_of(me*128,128),128)
-            return jnp.where(me==3,R,mat[mine,512:640]-mm(mat[mine,b:b+128],R))
+            return jnp.where(me==3,near,mat[mine,512:640]-mm(mat[mine,b:b+128],near))
         o=k+1
-        mat[128*o:128*o+128,128*o:128*o+128]-=mm(mat[128*o:128*o+128,b:b+128],R[:,:128])
-        mat[128*o:128*o+128,128*o+128:]-=mm(mat[128*o:128*o+128,b:b+128],R[:,128:])
+        mat[128*o:128*o+128,128*o:128*o+128]-=mm(mat[128*o:128*o+128,b:b+128],near)
+        away=mm(Mi,mat[b:b+128,b+256:])
+        mat[128*o:128*o+128,128*o+128:]-=mm(mat[128*o:128*o+128,b:b+128],away)
+        R=jnp.concatenate([near,away],axis=1)
         for o in range(4):
             if o not in (k,k+1):
                 mat[128*o:128*o+128,b+128:]-=mm(mat[128*o:128*o+128,b:b+128],R)

time: 54.8 us -> 54.9 us (level)
  no operation moved by 1% of the time
where the time goes in v9:
time: 54.9 us; the launch traced here: 54.7 us
  Pallas kernels  52.9 us (96%)
  local copies, waits for them, and re-layouts  1.19 us (2%)
  between operations  0.66 us (1%)
    pallas_call x1, Pallas kernels, fit(): pl.pallas_call(functools.partial(fit_kernel, (nx, ny, nz, piece), consts)...  52.9 us
    unnamed x1, local copies, waits for them, and re-layouts  1.19 us

profile of v9, /device:TPU:1, one launch (start us, length us, event | category | flops | bytes accessed | tf_op | source)
XLA Modules:
  0.0 54.7 jit_solution(17371968168752145529)
XLA Ops:
  0.7 52.9 %fit.1 = f32[1,128]{1,0:T(1,128)} custom-call(s32[1]{0:T(128)S(6)} %copy.7.bin_hbm, f32[1,2048]{1,0:T(1,128)} %p_hbm.1, s32[1,2048]{1,0:T(1,128)} %cyc_hbm.1, s32[1,2048]{1,0:T(1,128)} %az_hbm.1, s32[1,512]{1,0:T(1,128)} %bitcast.1), custom_call_target="tpu_custom_call" | custom-call | tf_op jit(solution)/shard_map/fit/pallas_call | solution.py:420
  53.5 1.2 %copy.8 = f32[1,128]{1,0:T(1,128)} copy(f32[1,128]{1,0:T(1,128)} %fit.1) | data formatting | bytes 1024
